TPU v7x, 128 devices: a whole 4x4x4 slice. The times are simulated.
128 devices in a mesh: ep: 32 (over x, z, core), edp: 4 (over y).
Axes of the slice: x: 4, y: 4, z: 4, core: 2. Of those that a mesh axis runs over, the one named last changes fastest.
Arguments:
- tokens: bfloat16 [24576, 3584], P(('ep', 'edp')), may hold values from -6 to 6
- upstream: bfloat16 [24576, 3584], P(('ep', 'edp')), may hold values from -3 to 3
- expert_ids: int32 [24576, 2], P(('ep', 'edp')), may hold values from 0 to 31, all different within a row; in each aligned block of 192 rows (0 to 191, 192 to 383, ...) at most 15 rows name the same one
- gate_values: bfloat16 [24576, 2], P(('ep', 'edp')), may hold values from 0.049804688 to 0.59765625
- w_gate: bfloat16 [32, 3584, 1024], P('ep', 'edp'), may hold values from -0.09375 to 0.09375
- w_up: bfloat16 [32, 3584, 1024], P('ep', 'edp'), may hold values from -0.09375 to 0.09375
- w_down: bfloat16 [32, 3584, 1024], P('ep', 'edp'), may hold values from -0.1875 to 0.1875
Outputs:
- token_grad: bfloat16 [24576, 3584], P(('ep', 'edp'))
- gate_grad: bfloat16 [24576, 2], P(('ep', 'edp'))
- grad_gate: bfloat16 [32, 3584, 1024], P('ep', 'edp')
- grad_up: bfloat16 [32, 3584, 1024], P('ep', 'edp')
- grad_down: bfloat16 [32, 3584, 1024], P('ep', 'edp')
Inputs may be any that keep to these rules, and one draw needn't show every extreme that they name: `expert_ids`: the 2 ids of a token differ. Among the rows of one device (aligned blocks of 192 tokens) no expert is named more than 15 times, and in every draw some device names some expert exactly 15 times.
All inputs are finite; a program needn't handle non-finite values.
Results may differ from a plain program's by a relative error of at most 0.013.
Values may be sent and summed in bfloat16 or wider, within the bound.
A program may use at most 192 MiB of HBM per device.

v0:
```python
import jax
import jax.numpy as jnp
from jax import lax
from jax.sharding import PartitionSpec as P


def expert_backward(x_rows, dy_rows, gate_rows, gate_w, up_w, down_w):
    pre_gate = jnp.dot(x_rows, gate_w, preferred_element_type=jnp.float32)
    pre_up = jnp.dot(x_rows, up_w, preferred_element_type=jnp.float32)
    back = jnp.dot(dy_rows, down_w, preferred_element_type=jnp.float32)
    sigma = jax.nn.sigmoid(pre_gate)
    silu_val = pre_gate * sigma
    act = (silu_val * pre_up).astype(jnp.bfloat16)
    act_f = act.astype(jnp.float32)
    gate_out = jnp.sum(act_f * back, axis=1).astype(jnp.bfloat16)
    weight_f = gate_rows.astype(jnp.float32)[:, None]
    d_act = weight_f * back
    d_gate_pre = (d_act * pre_up * sigma * (1.0 + pre_gate * (1.0 - sigma))).astype(jnp.bfloat16)
    d_up_pre = (d_act * silu_val).astype(jnp.bfloat16)
    scaled_act = (weight_f * act_f).astype(jnp.bfloat16)
    contract = (((1,), (1,)), ((), ()))
    reply = lax.dot_general(d_gate_pre, gate_w, contract, preferred_element_type=jnp.float32)
    reply = reply + lax.dot_general(d_up_pre, up_w, contract, preferred_element_type=jnp.float32)
    return (reply.astype(jnp.bfloat16), gate_out, d_gate_pre, d_up_pre, scaled_act)


def over_rows(left, right):
    return lax.dot_general(
        left, right, (((0,), (0,)), ((), ())), preferred_element_type=jnp.float32
    )


def three_terms(x_cols, dy_cols, d_gate_pre, d_up_pre, scaled_act):
    return jnp.concatenate(
        [
            over_rows(x_cols, d_gate_pre),
            over_rows(x_cols, d_up_pre),
            over_rows(dy_cols, scaled_act),
        ],
        axis=1,
    )


def shards(tokens, upstream, expert_ids, gate_values, w_gate, w_up, w_down):
    experts = lax.axis_size("ep")
    groups = lax.axis_size("edp")
    tok_count, top_count = expert_ids.shape
    model_width = tokens.shape[1]
    hidden_width = w_gate.shape[2]
    capacity = min(tok_count, 5 * tok_count * top_count // (4 * experts))
    buffer_rows = experts * capacity
    flat_ids = expert_ids.reshape(-1)
    onehot = (flat_ids[:, None] == jnp.arange(experts, dtype=jnp.int32)[None, :]).astype(jnp.int32)
    slot_idx = jnp.sum(jnp.cumsum(onehot, axis=0) * onehot, axis=1) - 1
    target = flat_ids * capacity + slot_idx
    assign = (jnp.arange(buffer_rows, dtype=jnp.int32)[:, None] == target[None, :]).astype(
        jnp.bfloat16
    )
    dispatch_map = jnp.sum(assign.reshape(buffer_rows, tok_count, top_count), axis=2)
    x_send = jnp.dot(dispatch_map, tokens, preferred_element_type=jnp.float32).astype(jnp.bfloat16)
    dy_send = jnp.dot(dispatch_map, upstream, preferred_element_type=jnp.float32).astype(
        jnp.bfloat16
    )
    gate_send = jnp.dot(
        assign, gate_values.reshape(-1, 1), preferred_element_type=jnp.float32
    ).astype(jnp.bfloat16)
    x_recv, dy_recv, gate_recv = (
        lax.all_to_all(
            x_send.reshape(experts, capacity, model_width),
            "ep",
            split_axis=0,
            concat_axis=0,
            tiled=True,
        ),
        lax.all_to_all(
            dy_send.reshape(experts, capacity, model_width),
            "ep",
            split_axis=0,
            concat_axis=0,
            tiled=True,
        ),
        lax.all_to_all(
            gate_send.reshape(experts, capacity), "ep", split_axis=0, concat_axis=0, tiled=True
        ),
    )
    x_rows = x_recv.reshape(buffer_rows, model_width)
    dy_rows = dy_recv.reshape(buffer_rows, model_width)
    gate_rows = gate_recv.reshape(buffer_rows)
    full_gate, full_up, full_down = (
        lax.all_gather(w_gate, "edp", axis=1, tiled=True),
        lax.all_gather(w_up, "edp", axis=1, tiled=True),
        lax.all_gather(w_down, "edp", axis=1, tiled=True),
    )
    reply, gate_out, d_gate_pre, d_up_pre, scaled_act = expert_backward(
        x_rows, dy_rows, gate_rows, full_gate[0], full_up[0], full_down[0]
    )
    back_rows, back_gate = (
        lax.all_to_all(
            reply.reshape(experts, capacity, model_width),
            "ep",
            split_axis=0,
            concat_axis=0,
            tiled=True,
        ),
        lax.all_to_all(
            gate_out.reshape(experts, capacity), "ep", split_axis=0, concat_axis=0, tiled=True
        ),
    )
    token_grad = over_rows(dispatch_map, back_rows.reshape(buffer_rows, model_width)).astype(
        jnp.bfloat16
    )
    gate_grad = (
        over_rows(assign, back_gate.reshape(buffer_rows, 1))
        .reshape(tok_count, top_count)
        .astype(jnp.bfloat16)
    )
    shard_rows = model_width // groups
    summed = lax.psum_scatter(
        three_terms(x_rows, dy_rows, d_gate_pre, d_up_pre, scaled_act).astype(jnp.bfloat16),
        "edp",
        scatter_dimension=0,
        tiled=True,
    )
    grad_gate = summed[:, :hidden_width].reshape(1, shard_rows, hidden_width)
    grad_up = summed[:, hidden_width : 2 * hidden_width].reshape(1, shard_rows, hidden_width)
    grad_down = summed[:, 2 * hidden_width :].reshape(1, shard_rows, hidden_width)
    return (token_grad, gate_grad, grad_gate, grad_up, grad_down)


def solution(mesh):
    in_specs = (
        P(("ep", "edp"), None),
        P(("ep", "edp"), None),
        P(("ep", "edp"), None),
        P(("ep", "edp"), None),
        P("ep", "edp", None),
        P("ep", "edp", None),
        P("ep", "edp", None),
    )
    out_specs = (
        P(("ep", "edp"), None),
        P(("ep", "edp"), None),
        P("ep", "edp", None),
        P("ep", "edp", None),
        P("ep", "edp", None),
    )
    return jax.shard_map(shards, mesh=mesh, in_specs=in_specs, out_specs=out_specs, check_vma=False)
```

profile of v0, /device:TPU:112, one launch (start us, length us, event | category | flops | bytes accessed | tf_op | source)
XLA Modules:
  0.0 529.7 jit_solution(7221206491593846405)
XLA Ops:
  7.2 0.7 all-gather.8.cloned.1.call-update
  8.0 0.7 all-gather.6.cloned.1.call-update
  8.7 0.7 all-gather.4.cloned.1.call-update
  10.2 0.9 reduce-window.6
  11.4 0.2 fusion.20
  11.7 0.7 all_to_all.25
  12.4 7.1 %all-to-all-start = ((bf16[32,1,15]{2,1,0:T(2,128)(2,1)}), bf16[32,1,15]{2,1,0:T(2,128)(2,1)S(1)}, u32[]{:S(2)}, u32[]{:S(2)}) async-start(bf16[32,1,15]{2,1,0:T(2,128)(2,1)} %all_to_all.25), calls=%async_computation | async-start | bytes 32768 | tf_op jit(solution)/shard_map/all_to_all | solution.py:82
  20.0 2.9 convolution_convert_fusion.3
  22.9 4.9 reshape.150
  27.8 7.5 %all-to-all-start.2 = ((bf16[32,15,3584]{2,1,0:T(8,128)(2,1)}), bf16[32,15,3584]{2,1,0:T(8,128)(2,1)}, u32[]{:S(2)}, u32[]{:S(2)}) async-start(bf16[32,15,3584]{2,1,0:T(8,128)(2,1)} %reshape.150), calls=%async_computation.2 | async-start | bytes 7340032 | tf_op jit(solution)/shard_map/all_to_all | solution.py:68
  35.4 2.8 convolution_convert_fusion.4
  38.2 4.8 reshape.148
  43.0 36.6 %all-to-all-done.2 = bf16[32,15,3584]{2,1,0:T(8,128)(2,1)} async-done(((bf16[32,15,3584]{2,1,0:T(8,128)(2,1)}), bf16[32,15,3584]{2,1,0:T(8,128)(2,1)}, u32[]{:S(2)}, u32[]{:S(2)}) %all-to-all-start.2) | async-done | bytes 3440672 | tf_op jit(solution)/shard_map/all_to_all | solution.py:68
  79.6 8.6 %all-to-all-start.1 = ((bf16[32,15,3584]{2,1,0:T(8,128)(2,1)}), bf16[32,15,3584]{2,1,0:T(8,128)(2,1)}, u32[]{:S(2)}, u32[]{:S(2)}) async-start(bf16[32,15,3584]{2,1,0:T(8,128)(2,1)} %reshape.148), calls=%async_computation.1 | async-start | bytes 7340032 | tf_op jit(solution)/shard_map/all_to_all | solution.py:75
  88.2 0.2 reduce-scatter.4.cloned.1.call-start
  88.6 4.8 reshape.151
  93.4 39.1 %all-to-all-done.1 = bf16[32,15,3584]{2,1,0:T(8,128)(2,1)} async-done(((bf16[32,15,3584]{2,1,0:T(8,128)(2,1)}), bf16[32,15,3584]{2,1,0:T(8,128)(2,1)}, u32[]{:S(2)}, u32[]{:S(2)}) %all-to-all-start.1) | async-done | bytes 3440672 | tf_op jit(solution)/shard_map/all_to_all | solution.py:75
  132.4 4.8 reshape.149
  137.3 9.2 %fusion.2 = f32[480,1024]{1,0:T(8,128)} fusion(bf16[480,3584]{1,0:T(8,128)(2,1)} %reshape.151, bf16[1,3584,1024]{2,1,0:T(8,128)(2,1)} %all-gather.8.cloned.1.call-done), kind=kOutput, calls=%fused_computation.6 | convolution fusion | flops 3523215360 | bytes 12746752 | tf_op jit(solution)/shard_map/dot_general | solution.py:8
  146.5 15.2 %all-gather.6.cloned.1.call-done = bf16[1,3584,1024]{2,1,0:T(8,128)(2,1)} async-done(((bf16[1,896,1024]{2,1,0:T(8,128)(2,1)}), bf16[1,3584,1024]{2,1,0:T(8,128)(2,1)}) %all-gather.6.cloned.1.call-update) | async-done | bytes 7340048 | tf_op jit(solution)/shard_map/all_gather | solution.py:91
  161.7 9.1 %fusion.6 = f32[480,1024]{1,0:T(8,128)} fusion(bf16[480,3584]{1,0:T(8,128)(2,1)} %reshape.151, bf16[1,3584,1024]{2,1,0:T(8,128)(2,1)} %all-gather.6.cloned.1.call-done), kind=kOutput, calls=%fused_computation.10 | convolution fusion | flops 3523215360 | bytes 12746752 | tf_op jit(solution)/shard_map/dot_general | solution.py:9
  170.9 67.8 %all-gather.4.cloned.1.call-done = bf16[1,3584,1024]{2,1,0:T(8,128)(2,1)} async-done(((bf16[1,896,1024]{2,1,0:T(8,128)(2,1)}), bf16[1,3584,1024]{2,1,0:T(8,128)(2,1)}) %all-gather.4.cloned.1.call-update) | async-done | bytes 7340048 | tf_op jit(solution)/shard_map/all_gather | solution.py:92
  238.6 9.9 %fusion.12 = (bf16[480]{0:T(512)(128)(2,1)S(1)}, bf16[480,1024]{1,0:T(8,128)(2,1)S(1)}, bf16[480,1024]{1,0:T(8,128)(2,1)S(1)}, bf16[480,1024]{1,0:T(8,128)(2,1)S(1)}) fusion(f32[480,1024]{1,0:T(8,128)} %fusion.6, f32[480,1024]{1,0:T(8,128)} %fusion.2, f32[480]{0:T(512)S(1)} %reshape.158, bf16[480,3584]{1,0:T(8,128)(2,1)} %reshape.149, ...), kind=kOutput, calls=%fused_computation.20 | convolution fusion | flops 3532553728 | bytes 17664832 | tf_op jit(solution)/shard_map/dot_general | solution.py:10
  248.6 6.2 %convolution_convert_fusion = bf16[3584,1024]{0,1:T(8,128)(2,1)} fusion(bf16[480,3584]{1,0:T(8,128)(2,1)S(1)} %copy-done.3, bf16[480,1024]{1,0:T(8,128)(2,1)S(1)} %get-tuple-element.31, f32[480]{0:T(512)S(1)} %reshape.158), kind=kOutput, calls=%fused_computation.1 | convolution fusion | flops 3528359936 | bytes 11765632 | tf_op jit(solution)/shard_map/dot_general | solution.py:28
  254.8 6.1 %convolution_convert_fusion.2 = bf16[3584,1024]{0,1:T(8,128)(2,1)} fusion(bf16[480,3584]{1,0:T(8,128)(2,1)S(1)} %copy-done.2, bf16[480,1024]{1,0:T(8,128)(2,1)S(1)} %get-tuple-element.32), kind=kOutput, calls=%fused_computation.3 | convolution fusion | flops 3526885376 | bytes 11763712 | tf_op jit(solution)/shard_map/dot_general | solution.py:28
  260.9 6.2 %convolution_convert_fusion.1 = bf16[3584,1024]{0,1:T(8,128)(2,1)} fusion(bf16[480,3584]{1,0:T(8,128)(2,1)S(1)} %copy-done.2, bf16[480,1024]{1,0:T(8,128)(2,1)S(1)} %get-tuple-element.36), kind=kOutput, calls=%fused_computation.2 | convolution fusion | flops 3526885376 | bytes 11763712 | tf_op jit(solution)/shard_map/dot_general | solution.py:28
  267.0 15.6 %pad_maximum_fusion = bf16[3584,3072]{0,1:T(8,128)(2,1)} fusion(bf16[3584,1024]{0,1:T(8,128)(2,1)} %convolution_convert_fusion, bf16[3584,1024]{0,1:T(8,128)(2,1)} %convolution_convert_fusion.1, bf16[3584,1024]{0,1:T(8,128)(2,1)} %convolution_convert_fusion.2), kind=kLoop, calls=%fused_computation | loop fusion | flops 66060288 | bytes 44040192 | tf_op jit(solution)/shard_map/concatenate | solution.py:34
  282.7 28.6 %copy.60 = bf16[3584,3072]{1,0:T(8,128)(2,1)} copy(bf16[3584,3072]{0,1:T(8,128)(2,1)} %pad_maximum_fusion) | data formatting | bytes 44040192
  311.3 0.7 convert_element_type.88
  312.1 7.3 %all-to-all-start.4 = ((bf16[32,1,15]{2,1,0:T(2,128)(2,1)}), bf16[32,1,15]{2,1,0:T(2,128)(2,1)S(1)}, u32[]{:S(2)}, u32[]{:S(2)}) async-start(bf16[32,1,15]{2,1,0:T(2,128)(2,1)} %convert_element_type.88), calls=%async_computation.4 | async-start | bytes 32768 | tf_op jit(solution)/shard_map/all_to_all | solution.py:105
  319.3 6.5 %fusion = f32[480,3584]{1,0:T(8,128)S(1)} fusion(bf16[480,1024]{1,0:T(8,128)(2,1)} %copy-done.7, bf16[1,3584,1024]{2,1,0:T(8,128)(2,1)} %all-gather.8.cloned.1.call-done), kind=kOutput, calls=%fused_computation.4 | convolution fusion | flops 3523215360 | bytes 15204352 | tf_op jit(solution)/shard_map/dot_general | solution.py:22
  325.9 8.8 %add_convert_fusion = bf16[480,3584]{1,0:T(8,128)(2,1)} fusion(f32[480,3584]{1,0:T(8,128)S(1)} %fusion, bf16[480,1024]{1,0:T(8,128)(2,1)S(1)} %get-tuple-element.36, bf16[1,3584,1024]{2,1,0:T(8,128)(2,1)} %all-gather.6.cloned.1.call-done), kind=kOutput, calls=%fused_computation.14 | convolution fusion | flops 3526656000 | bytes 18644992 | tf_op jit(solution)/shard_map/dot_general | solution.py:23
  334.7 4.8 reshape.152
  339.5 7.6 %all-to-all-start.3 = ((bf16[32,15,3584]{2,1,0:T(8,128)(2,1)}), bf16[32,15,3584]{2,1,0:T(8,128)(2,1)}, u32[]{:S(2)}, u32[]{:S(2)}) async-start(bf16[32,15,3584]{2,1,0:T(8,128)(2,1)} %reshape.152), calls=%async_computation.3 | async-start | bytes 7340032 | tf_op jit(solution)/shard_map/all_to_all | solution.py:98
  347.3 0.3 eq.77
  347.7 0.2 fusion.18
  348.0 0.7 copy.59
  348.7 42.7 %all-to-all-done.3 = bf16[32,15,3584]{2,1,0:T(8,128)(2,1)} async-done(((bf16[32,15,3584]{2,1,0:T(8,128)(2,1)}), bf16[32,15,3584]{2,1,0:T(8,128)(2,1)}, u32[]{:S(2)}, u32[]{:S(2)}) %all-to-all-start.3) | async-done | bytes 3440672 | tf_op jit(solution)/shard_map/all_to_all | solution.py:98
  391.4 4.8 reshape.153
  396.2 3.9 convolution_convert_fusion.5
  400.1 101.3 %reduce-scatter.4.cloned.1.call-done = bf16[896,3072]{1,0:T(8,128)(2,1)} async-done(((bf16[3584,3072]{1,0:T(8,128)(2,1)}), bf16[896,3072]{1,0:T(8,128)(2,1)}) %reduce-scatter.4.cloned.1.call-update) | async-done | bytes 5505040
  501.5 5.2 fusion.26
  506.7 3.1 copy.64
  509.7 2.4 copy.57
  512.1 3.1 copy.63
  515.2 2.4 copy.56
  517.6 3.2 copy.62
  520.8 2.4 copy.55
  (43 shorter events, 2.1 us)
Async XLA Ops:
  7.2 12.8 %copy-start = (bf16[192,3584]{1,0:T(8,128)(2,1)S(1)}, bf16[192,3584]{1,0:T(8,128)(2,1)}, u32[]{:S(2)}) copy-start(bf16[192,3584]{1,0:T(8,128)(2,1)} %param.7) | copy-start | bytes 4128772
  7.2 2.2 copy-start.5
  7.2 2.7 copy-start.6
  7.2 130.1 %all-gather.8.cloned.1.call-start = ((), (), s32[]{:S(2)}) async-start(), calls=%async_computation.8 | async-start | bytes 9175040 | tf_op jit(solution)/shard_map/all_gather | solution.py:90
  7.9 153.8 %all-gather.6.cloned.1.call-start = ((), (), s32[]{:S(2)}) async-start(), calls=%async_computation.7 | async-start | bytes 9175040 | tf_op jit(solution)/shard_map/all_gather | solution.py:91
  8.7 229.9 %all-gather.4.cloned.1.call-start = ((), (), s32[]{:S(2)}) async-start(), calls=%async_computation.6 | async-start | bytes 9175040 | tf_op jit(solution)/shard_map/all_gather | solution.py:92
  12.4 15.4 %all-to-all-start = ((bf16[32,1,15]{2,1,0:T(2,128)(2,1)}), bf16[32,1,15]{2,1,0:T(2,128)(2,1)S(1)}, u32[]{:S(2)}, u32[]{:S(2)}) async-start(bf16[32,1,15]{2,1,0:T(2,128)(2,1)} %all_to_all.25), calls=%async_computation | async-start | bytes 32768 | tf_op jit(solution)/shard_map/all_to_all | solution.py:82
  27.8 7.6 %copy-start.4 = (bf16[192,3584]{1,0:T(8,128)(2,1)S(1)}, bf16[192,3584]{1,0:T(8,128)(2,1)}, u32[]{:S(2)}) copy-start(bf16[192,3584]{1,0:T(8,128)(2,1)} %param.8) | copy-start | bytes 4128772
  27.8 51.8 %all-to-all-start.2 = ((bf16[32,15,3584]{2,1,0:T(8,128)(2,1)}), bf16[32,15,3584]{2,1,0:T(8,128)(2,1)}, u32[]{:S(2)}, u32[]{:S(2)}) async-start(bf16[32,15,3584]{2,1,0:T(8,128)(2,1)} %reshape.150), calls=%async_computation.2 | async-start | bytes 7340032 | tf_op jit(solution)/shard_map/all_to_all | solution.py:68
  79.6 52.8 %all-to-all-start.1 = ((bf16[32,15,3584]{2,1,0:T(8,128)(2,1)}), bf16[32,15,3584]{2,1,0:T(8,128)(2,1)}, u32[]{:S(2)}, u32[]{:S(2)}) async-start(bf16[32,15,3584]{2,1,0:T(8,128)(2,1)} %reshape.148), calls=%async_computation.1 | async-start | bytes 7340032 | tf_op jit(solution)/shard_map/all_to_all | solution.py:75
  88.2 413.3 %reduce-scatter.4.cloned.1.call-start = ((), (), s32[]{:S(2)}) async-start(), calls=%async_computation.9 | async-start | bytes 27525120
  238.6 9.9 %copy-start.3 = (bf16[480,3584]{1,0:T(8,128)(2,1)S(1)}, bf16[480,3584]{1,0:T(8,128)(2,1)}, u32[]{:S(2)}) copy-start(bf16[480,3584]{1,0:T(8,128)(2,1)} %reshape.149) | copy-start | bytes 10321924
  248.5 6.3 %copy-start.7 = (bf16[480,1024]{1,0:T(8,128)(2,1)}, bf16[480,1024]{1,0:T(8,128)(2,1)S(1)}, u32[]{:S(2)}) copy-start(bf16[480,1024]{1,0:T(8,128)(2,1)S(1)} %get-tuple-element.32) | copy-start | bytes 2949124
  248.6 6.2 %copy-start.2 = (bf16[480,3584]{1,0:T(8,128)(2,1)S(1)}, bf16[480,3584]{1,0:T(8,128)(2,1)}, u32[]{:S(2)}) copy-start(bf16[480,3584]{1,0:T(8,128)(2,1)} %reshape.151) | copy-start | bytes 10321924
  312.1 27.5 %all-to-all-start.4 = ((bf16[32,1,15]{2,1,0:T(2,128)(2,1)}), bf16[32,1,15]{2,1,0:T(2,128)(2,1)S(1)}, u32[]{:S(2)}, u32[]{:S(2)}) async-start(bf16[32,1,15]{2,1,0:T(2,128)(2,1)} %convert_element_type.88), calls=%async_computation.4 | async-start | bytes 32768 | tf_op jit(solution)/shard_map/all_to_all | solution.py:105
  339.5 51.8 %all-to-all-start.3 = ((bf16[32,15,3584]{2,1,0:T(8,128)(2,1)}), bf16[32,15,3584]{2,1,0:T(8,128)(2,1)}, u32[]{:S(2)}, u32[]{:S(2)}) async-start(bf16[32,15,3584]{2,1,0:T(8,128)(2,1)} %reshape.152), calls=%async_computation.3 | async-start | bytes 7340032 | tf_op jit(solution)/shard_map/all_to_all | solution.py:98
  517.6 5.6 %copy-start.1 = (bf16[192,3584]{1,0:T(8,128)(2,1)S(1)}, bf16[192,3584]{1,0:T(8,128)(2,1)}, u32[]{:S(2)}) copy-start(bf16[192,3584]{1,0:T(8,128)(2,1)} %param.7) | copy-start | bytes 4128772
Sparse Core Ops, SparseCore 0:
  9.7 75.0 all-gather.7
  86.5 75.2 all-gather.5
  163.4 75.2 all-gather.3
  311.5 189.9 reduce-scatter.3
where the time goes:
time: 535 us; the launch traced here: 530 us
  waiting for transfers between devices  305 us (57%)
  local copies, waits for them, and re-layouts  83.1 us (16%)
  matrix products  72.3 us (14%)
  starting transfers between devices  38.4 us (7%)
  other arithmetic  17.1 us (3%)
  between operations  14 us (3%)
    unnamed x5, waiting for transfers between devices  103 us
    all_gather x1, waiting for transfers between devices, shards(): lax.all_gather(w_down, 'edp', axis=1, tiled=True)  67.8 us
    unnamed x25, local copies, waits for them, and re-layouts  45.4 us
    all_to_all x1, waiting for transfers between devices, shards(): lax.all_to_all(reply.reshape(experts, capacity, model_width), 'ep', split...  42.7 us
    all_to_all x1, waiting for transfers between devices, shards(): lax.all_to_all(dy_send.reshape(experts, capacity, model_width), 'ep', spl...  39.1 us
    all_to_all x1, waiting for transfers between devices, shards(): lax.all_to_all(x_send.reshape(experts, capacity, model_width), 'ep', spli...  36.6 us
    dot_general x5, matrix products, over_rows(): lax.dot_general(left, right, (((0,), (0,)), ((), ())), preferred_element_...  22.7 us
    concatenate x1, other arithmetic, three_terms(): jnp.concatenate([over_rows(x_cols, d_gate_pre), over_rows(x_cols, d_up_pr...  15.6 us
  transfers between devices with their start and end apart: 9, of which 6 were waited for; matrix products, arithmetic and copies ran while one was open for 15% of the time, Pallas kernels for 0%

commit v1 on v0

v1 whole, which is shorter than its diff:
```python
import functools

import jax
import jax.numpy as jnp
from jax import lax
from jax.experimental import pallas as pl
from jax.experimental.pallas import tpu as pltpu
from jax.sharding import PartitionSpec as P

MESH = pl.DeviceIdType.MESH
ROWS = 16


def place():
    ep, plane = lax.axis_index("ep"), lax.axis_index("edp")
    core = lax.rem(ep, 2)
    parity = plane // 2
    beside = plane + 1 - 2 * lax.rem(plane, 2)
    across = 3 - plane
    return ep, ep // 2, core, plane, parity, beside, across


def remote(src, dst, send, recv, ep, plane):
    return pltpu.make_async_remote_copy(
        src_ref=src, dst_ref=dst, send_sem=send, recv_sem=recv,
        device_id=(ep, plane), device_id_type=MESH,
    )


def landed(ref, sem):
    pltpu.make_async_copy(ref, ref, sem).wait()


def gather_kernel(chips, x_send, dy_send, w_gate, w_up, w_down, x_all, dy_all, f_gate, f_up, f_down,
                  local_sem, token_send, token_recv, pass_send, pass_recv,
                  weight_send, weight_recv, relay_send):
    ep, chip, core, plane, parity, beside, across = place()
    depth, width = w_gate.shape
    half = width // 2
    sibling = ep + 1 - 2 * core
    shards = (w_gate, w_up, w_down)
    fulls = (f_gate, f_up, f_down)

    def rows_of(ref, shard):
        return ref.at[pl.ds(pl.multiple_of(shard * depth, 16), depth)]

    def columns(ref, part):
        return ref.at[:, pl.ds(pl.multiple_of(part * half, 128), half)]

    away = core != parity
    for m in range(3):
        @pl.when(away)
        def _(m=m):
            for part in range(2):
                remote(columns(shards[m], part), rows_of(fulls[m], plane), weight_send.at[m, part],
                       weight_recv.at[m, 0], 2 * chip + part, across).start()

    for n, (source, target) in enumerate(((x_send, x_all), (dy_send, dy_all))):
        for group in range(2):
            def send(k, carry, n=n, group=group, source=source, target=target):
                to = lax.rem(chip + k, chips)
                to_plane = plane if group == 0 else across
                kind = parity if group == 0 else 1 - parity
                remote(source.at[2 * to + kind], target.at[core, group, chip], token_send.at[n, group],
                       token_recv.at[n, group], 2 * to + core, to_plane).start()
                return carry

            if group == 0:
                pltpu.make_async_copy(source.at[2 * chip + parity], target.at[core, 0, chip],
                                      token_recv.at[n, 0]).start()
            lax.fori_loop(1 if group == 0 else 0, chips, send, 0)
        if n == 0:
            for m in range(3):
                @pl.when(jnp.logical_not(away))
                def _(m=m):
                    for part in range(2):
                        remote(columns(shards[m], part), rows_of(fulls[m], plane), weight_send.at[m, part],
                               weight_recv.at[m, 1], 2 * chip + part, beside).start()
                    pltpu.make_async_copy(columns(shards[m], core), rows_of(fulls[m], plane),
                                          weight_recv.at[m, 2]).start()
                    remote(columns(shards[m], 1 - core), rows_of(fulls[m], plane), weight_send.at[m, 2],
                           weight_recv.at[m, 2], sibling, plane).start()

    def relay(m):
        return remote(rows_of(fulls[m], across), rows_of(fulls[m], across), relay_send.at[m],
                      weight_recv.at[m, 3], 2 * chip + core, beside)

    def hand_over(n, group):
        target = (x_all, dy_all)[n]
        return remote(target.at[core, group], target.at[core, group], pass_send.at[n, group],
                      pass_recv.at[n, group], sibling, plane)

    for m in range(2):
        landed(rows_of(fulls[m], across), weight_recv.at[m, 0])
        relay(m).start()
    for group in range(2):
        landed(x_all.at[core, group], token_recv.at[0, group])
        hand_over(0, group).start()
    landed(rows_of(fulls[2], across), weight_recv.at[2, 0])
    relay(2).start()
    for group in range(2):
        landed(dy_all.at[core, group], token_recv.at[1, group])
        hand_over(1, group).start()

    for m in range(3):
        landed(rows_of(fulls[m], beside), weight_recv.at[m, 1])
        landed(rows_of(fulls[m], plane), weight_recv.at[m, 2])
        landed(rows_of(fulls[m], 3 - beside), weight_recv.at[m, 3])
        relay(m).wait_send()
        for part in range(2):
            landed(columns(shards[m], part), weight_send.at[m, part])

        @pl.when(jnp.logical_not(away))
        def _(m=m):
            landed(columns(shards[m], 0), weight_send.at[m, 2])
    for n, target in enumerate((x_all, dy_all)):
        for group in range(2):
            hand_over(n, group).wait_send()
            landed(target.at[1 - core, group], pass_recv.at[n, group])
        landed(target.at[core, 0, pl.ds(0, chips - 1)], token_send.at[n, 0])
        landed(target.at[core, 1], token_send.at[n, 1])


def return_kernel(chips, reply, gates, t_gate, t_up, t_down, reply_out, gates_out, g_gate, g_up, g_down,
                  reply_own, reply_in, gates_own, gates_in, sums, arrived,
                  local_sem, pass_send, pass_recv, sum_send, sum_recv, out_send, out_recv,
                  back_send, back_recv):
    ep, chip, core, plane, parity, beside, across = place()
    width = g_gate.shape[1]
    half = width // 2
    sibling = ep + 1 - 2 * core
    terms = (t_gate, t_up, t_down)
    outs = (g_gate, g_up, g_down)

    def columns(ref, part):
        return ref.at[:, pl.ds(pl.multiple_of(part * half, 128), half)]

    passes = [
        remote(reply.at[1 - core], reply_in, pass_send.at[0], pass_recv.at[0], sibling, plane),
        remote(gates.at[1 - core], gates_in, pass_send.at[1], pass_recv.at[1], sibling, plane),
    ]
    loads = [
        pltpu.make_async_copy(reply.at[core], reply_own, local_sem.at[0]),
        pltpu.make_async_copy(gates.at[core], gates_own, local_sem.at[1]),
    ]
    for copy in passes + loads:
        copy.start()
    moves = {}
    for s in (1, 0):
        for m in range(3):
            theirs = 3 - beside if s else beside
            mine = across if s else plane
            moves[m, s] = (
                remote(terms[m].at[theirs], arrived.at[m, s], sum_send.at[m, s], sum_recv.at[m, s],
                       2 * chip + core, beside),
                pltpu.make_async_copy(terms[m].at[mine], sums.at[m, s], local_sem.at[2 + 2 * m + s]),
            )
            for copy in moves[m, s]:
                copy.start()

    for copy in loads:
        copy.wait()
    for copy in passes:
        copy.wait()

    def add_reply(k, carry):
        group, row = k // chips, lax.rem(k, chips)
        total = reply_own[group, row].astype(jnp.float32) + reply_in[group, row].astype(jnp.float32)
        reply_own[group, row] = total.astype(reply_own.dtype)
        gates_own[group, row] = gates_own[group, row] + gates_in[group, row]
        return carry

    lax.fori_loop(0, 2 * chips, add_reply, 0)
    for group in range(2):
        def send(k, carry, group=group):
            to = lax.rem(chip + k, chips)
            to_plane = plane if group == 0 else across
            remote(reply_own.at[group, to], reply_out.at[2 * chip + parity], back_send.at[0, group],
                   back_recv.at[0, group], 2 * to + core, to_plane).start()
            remote(gates_own.at[group, to], gates_out.at[2 * chip + parity], back_send.at[1, group],
                   back_recv.at[1, group], 2 * to + core, to_plane).start()
            return carry

        if group == 0:
            pltpu.make_async_copy(reply_own.at[0, chip], reply_out.at[2 * chip + parity],
                                  back_recv.at[0, 0]).start()
            pltpu.make_async_copy(gates_own.at[0, chip], gates_out.at[2 * chip + parity],
                                  back_recv.at[1, 0]).start()
        lax.fori_loop(1 if group == 0 else 0, chips, send, 0)

    for s in (1, 0):
        for m in range(3):
            for copy in moves[m, s]:
                copy.wait()
            step = 128

            def add(k, carry, m=m, s=s):
                rows = pl.ds(pl.multiple_of(k * step, step), step)
                total = sums[m, s, rows].astype(jnp.float32) + arrived[m, s, rows].astype(jnp.float32)
                sums[m, s, rows] = total.astype(sums.dtype)
                return carry

            lax.fori_loop(0, sums.shape[2] // step, add, 0)
            if s:
                remote(sums.at[m, 1], columns(outs[m], core), out_send.at[m, 1], out_recv.at[m, core],
                       2 * chip + parity, across).start()
            else:
                @pl.when(core == parity)
                def _(m=m):
                    pltpu.make_async_copy(sums.at[m, 0], columns(outs[m], core), out_recv.at[m, core]).start()

                @pl.when(core != parity)
                def _(m=m):
                    remote(sums.at[m, 0], columns(outs[m], core), out_send.at[m, 0], out_recv.at[m, core],
                           2 * chip + parity, plane).start()

    for m in range(3):
        landed(sums.at[m, 1], out_send.at[m, 1])

        @pl.when(core != parity)
        def _(m=m):
            landed(sums.at[m, 0], out_send.at[m, 0])
        for part in range(2):
            landed(columns(outs[m], part), out_recv.at[m, part])
    for n, (own, out) in enumerate(((reply_own, reply_out), (gates_own, gates_out))):
        landed(own.at[0, pl.ds(0, chips - 1)], back_send.at[n, 0])
        landed(own.at[1], back_send.at[n, 1])
        for group in range(2):
            landed(own.at[group], back_recv.at[n, group])


def expert_backward(x_rows, dy_rows, gate_w, up_w, down_w):
    pre_gate = jnp.dot(x_rows, gate_w, preferred_element_type=jnp.float32)
    pre_up = jnp.dot(x_rows, up_w, preferred_element_type=jnp.float32)
    back = jnp.dot(dy_rows, down_w, preferred_element_type=jnp.float32)
    sigma = jax.nn.sigmoid(pre_gate)
    silu_val = pre_gate * sigma
    act = (silu_val * pre_up).astype(jnp.bfloat16)
    gate_out = jnp.sum(act.astype(jnp.float32) * back, axis=1, keepdims=True)
    d_gate_pre = (back * pre_up * sigma * (1.0 + pre_gate * (1.0 - sigma))).astype(jnp.bfloat16)
    d_up_pre = (back * silu_val).astype(jnp.bfloat16)
    contract = (((1,), (1,)), ((), ()))
    reply = lax.dot_general(d_gate_pre, gate_w, contract, preferred_element_type=jnp.float32)
    reply = reply + lax.dot_general(d_up_pre, up_w, contract, preferred_element_type=jnp.float32)
    return reply.astype(jnp.bfloat16), gate_out, d_gate_pre, d_up_pre, act


def over_rows(left, right):
    return lax.dot_general(left, right, (((0,), (0,)), ((), ())), preferred_element_type=jnp.float32)


def shards(tokens, upstream, expert_ids, gate_values, w_gate, w_up, w_down):
    experts = lax.axis_size("ep")
    chips = experts // 2
    tok_count, top_count = expert_ids.shape
    model_width = tokens.shape[1]
    depth, width = w_gate.shape[1:]
    half = width // 2
    buffer_rows = experts * ROWS
    bf16 = jnp.bfloat16
    flat_ids = expert_ids.reshape(-1)
    onehot = (flat_ids[:, None] == jnp.arange(experts, dtype=jnp.int32)[None, :]).astype(jnp.int32)
    slot_idx = jnp.sum(jnp.cumsum(onehot, axis=0) * onehot, axis=1) - 1
    target = (flat_ids * ROWS + slot_idx).reshape(tok_count, top_count)
    slots = jnp.arange(buffer_rows, dtype=jnp.int32)
    picks = [slots[:, None] == target[None, :, k] for k in range(top_count)]
    zero = jnp.zeros((), bf16)
    dispatch_map = sum(pick.astype(bf16) for pick in picks)
    scaled_map = sum(jnp.where(pick, gate_values[None, :, k], zero) for k, pick in enumerate(picks))
    x_send = jnp.dot(dispatch_map, tokens, preferred_element_type=jnp.float32).astype(bf16)
    dy_send = jnp.dot(scaled_map, upstream, preferred_element_type=jnp.float32).astype(bf16)

    anywhere = pl.BlockSpec(memory_space=pl.ANY)
    dma = pltpu.SemaphoreType.DMA
    rows_shape = jax.ShapeDtypeStruct((2, 2, chips, ROWS, model_width), bf16)
    full_shape = jax.ShapeDtypeStruct((4 * depth, half), bf16)
    x_all, dy_all, f_gate, f_up, f_down = pl.pallas_call(
        functools.partial(gather_kernel, chips),
        out_shape=[rows_shape] * 2 + [full_shape] * 3,
        in_specs=[anywhere] * 5,
        out_specs=[anywhere] * 5,
        scratch_shapes=[dma((2,)), dma((2, 2)), dma((2, 2)), dma((2, 2)), dma((2, 2)),
                        dma((3, 3)), dma((3, 4)), dma((3,))],
        compiler_params=pltpu.CompilerParams(has_side_effects=True),
        name="gather_rows",
    )(x_send.reshape(experts, ROWS, model_width), dy_send.reshape(experts, ROWS, model_width),
      w_gate[0], w_up[0], w_down[0])

    x_rows = x_all.reshape(4 * chips * ROWS, model_width)
    dy_rows = dy_all.reshape(4 * chips * ROWS, model_width)
    reply, gate_out, d_gate_pre, d_up_pre, act = expert_backward(x_rows, dy_rows, f_gate, f_up, f_down)
    terms = [over_rows(left, right).astype(bf16).reshape(4, depth, half)
             for left, right in ((x_rows, d_gate_pre), (x_rows, d_up_pre), (dy_rows, act))]
    gates = jnp.broadcast_to(gate_out, (4 * chips * ROWS, 128))

    grad_shape = jax.ShapeDtypeStruct((depth, width), bf16)
    reply_out, gates_out, g_gate, g_up, g_down = pl.pallas_call(
        functools.partial(return_kernel, chips),
        out_shape=[jax.ShapeDtypeStruct((experts, ROWS, model_width), bf16),
                   jax.ShapeDtypeStruct((experts, ROWS, 128), jnp.float32)] + [grad_shape] * 3,
        in_specs=[anywhere] * 5,
        out_specs=[anywhere] * 5,
        scratch_shapes=[
            pltpu.VMEM((2, chips, ROWS, model_width), bf16), pltpu.VMEM((2, chips, ROWS, model_width), bf16),
            pltpu.VMEM((2, chips, ROWS, 128), jnp.float32), pltpu.VMEM((2, chips, ROWS, 128), jnp.float32),
            pltpu.VMEM((3, 2, depth, half), bf16), pltpu.VMEM((3, 2, depth, half), bf16),
            dma((8,)), dma((2,)), dma((2,)), dma((3, 2)), dma((3, 2)), dma((3, 2)), dma((3, 2)),
            dma((2, 2)), dma((2, 2))],
        compiler_params=pltpu.CompilerParams(has_side_effects=True, vmem_limit_bytes=48 << 20),
        name="return_rows",
    )(reply.reshape(2, 2, chips, ROWS, model_width), gates.reshape(2, 2, chips, ROWS, 128), *terms)

    token_grad = over_rows(dispatch_map, reply_out.reshape(buffer_rows, model_width)).astype(bf16)
    gate_rows = gates_out.reshape(buffer_rows, 128)[:, 0]
    gate_grad = jnp.stack([jnp.sum(jnp.where(pick, gate_rows[:, None], 0.0), axis=0) for pick in picks], axis=1)
    gate_grad = (gate_grad / gate_values.astype(jnp.float32)).astype(bf16)
    return token_grad, gate_grad, g_gate[None], g_up[None], g_down[None]


def solution(mesh):
    tokens_spec, weights_spec = P(("ep", "edp"), None), P("ep", "edp", None)
    return jax.shard_map(
        shards, mesh=mesh,
        in_specs=(tokens_spec,) * 4 + (weights_spec,) * 3,
        out_specs=(tokens_spec,) * 2 + (weights_spec,) * 3,
        check_vma=False,
    )
```

time: 535 us -> 391 us (0.73)
  waiting for transfers between devices: 305 us -> 0 us
  Pallas kernels: 0 us -> 301 us
  local copies, waits for them, and re-layouts: 83.1 us -> 7.72 us
  starting transfers between devices: 38.4 us -> 0 us
  other arithmetic: 17.1 us -> 2.57 us
  between operations: 14 us -> 0.77 us
    pallas_call x0 -> x2, Pallas kernels: none -> 301 us  [the longest x1 156 us: shards(): pl.pallas_call(functools.partial(gather_kernel, chips), out_shape=[rows_s...]
    all_to_all x5 -> x0, waiting for transfers between devices: 118 us -> none  [the longest x1 42.7 us: shards(): lax.all_to_all(reply.reshape(experts, capacity, model_width), 'ep', split...]
    unnamed x5 -> x0, waiting for transfers between devices: 103 us -> none
    all_gather x3 -> x0, waiting for transfers between devices: 83 us -> none  [the longest x1 67.8 us: shards(): lax.all_gather(w_down, 'edp', axis=1, tiled=True)]
    unnamed x25, local copies, waits for them, and re-layouts: 45.4 us -> 5.96 us
    all_to_all x5 -> x0, starting transfers between devices: 38.1 us -> none  [the longest x1 8.56 us: shards(): lax.all_to_all(dy_send.reshape(experts, capacity, model_width), 'ep', spl...]
    reshape x6 -> x0, local copies, waits for them, and re-layouts: 29 us -> none  [the longest x1 4.9 us: shards(): x_send.reshape(experts, capacity, model_width)]
    concatenate x1 -> x0, other arithmetic: 15.6 us -> none  [three_terms(): jnp.concatenate([over_rows(x_cols, d_gate_pre), over_rows(x_cols, d_up_pr...]
  transfers between devices with their start and end apart: 9 -> 0, of which waited for: 6 -> 0; matrix products, arithmetic and copies ran while one was open for 15% -> 0% of each run, Pallas kernels for 0% -> 0%
where the time goes in v1:
time: 391 us; the launch traced here: 384 us
  Pallas kernels  301 us (77%)
  matrix products  72.4 us (19%)
  local copies, waits for them, and re-layouts  7.72 us (2%)
    pallas_call x1, Pallas kernels, shards(): pl.pallas_call(functools.partial(gather_kernel, chips), out_shape=[rows_s...  156 us
    pallas_call x1, Pallas kernels, shards(): pl.pallas_call(functools.partial(return_kernel, chips), out_shape=[jax.Sh...  145 us
    dot_general x4, matrix products, over_rows(): lax.dot_general(left, right, (((0,), (0,)), ((), ())), preferred_element_...  23.9 us
    dot_general x1, matrix products, expert_backward(): back = jnp.dot(dy_rows, down_w, preferred_element_type=jnp.float32)  10.6 us
    dot_general x1, matrix products, expert_backward(): pre_gate = jnp.dot(x_rows, gate_w, preferred_element_type=jnp.float32)  9.64 us
    dot_general x1, matrix products, expert_backward(): lax.dot_general(d_up_pre, up_w, contract, preferred_element_type=jnp.floa...  9.34 us

profile of v1, /device:TPU:112, one launch (start us, length us, event | category | flops | bytes accessed | tf_op | source)
XLA Modules:
  0.0 384.2 jit_solution(15804519821377025558)
XLA Ops:
  0.6 0.0 copy-start
  0.6 0.9 copy.30
  1.6 0.1 eq.60
  1.7 0.9 reduce-window.6
  2.6 0.2 slice_reduce_fusion
  2.9 0.1 eq.56
  3.0 0.1 fusion.21
  3.1 0.1 sub.10
  3.3 0.1 copy.33
  3.3 0.7 multiply_add_fusion
  4.0 0.8 slice_reduce_fusion.2
  4.8 0.0 copy-done
  4.8 3.1 convolution_convert_fusion.3
  7.9 0.0 copy-done.5
  7.9 3.0 convolution_convert_fusion.4
  11.0 155.9 %gather_rows.1 = (bf16[2,2,16,16,3584]{4,3,2,1,0:T(8,128)(2,1)}, bf16[2,2,16,16,3584]{4,3,2,1,0:T(8,128)(2,1)}, bf16[3584,512]{1,0:T(8,128)(2,1)}, bf16[3584,512]{1,0:T(8,128)(2,1)}, bf16[3584,512]{1,0:T(8,128)(2,1)}) custom-call(bf16[32,16,3584]{2,1,0:T(8,128)(2,1)} %bitcast.61, bf16[32,16,3584]{2,1,0:T(8,128)(2,1)} %bitcast.60, ...), custom_call_target="tpu_custom_call" | custom-call | tf_op jit(solution)/shard_map/gather_rows/pallas_call | solution.py:277
  166.9 0.0 copy-start.7
  166.9 0.0 copy-start.8
  166.9 9.6 %fusion.27 = f32[1024,512]{0,1:T(8,128)} fusion(bf16[1024,3584]{1,0:T(8,128)(2,1)} %bitcast.83, bf16[3584,512]{1,0:T(8,128)(2,1)} %get-tuple-element.19), kind=kOutput, calls=%fused_computation.49 | convolution fusion | flops 3758096384 | bytes 13107200 | tf_op jit(solution)/shard_map/dot_general | solution.py:233
  176.5 0.0 copy-done.7
  176.5 0.0 copy-done.8
  176.5 5.4 %fusion.26 = f32[1024,512]{0,1:T(8,128)} fusion(bf16[1024,3584]{1,0:T(8,128)(2,1)S(1)} %bitcast.84, bf16[3584,512]{1,0:T(8,128)(2,1)S(1)} %copy-done.8), kind=kOutput, calls=%fused_computation.48 | convolution fusion | flops 3758096384 | bytes 13107200 | tf_op jit(solution)/shard_map/dot_general | solution.py:234
  181.9 10.6 %multiply_reduce_fusion = (f32[1024]{0:T(1024)S(1)}, bf16[1024,512]{0,1:T(8,128)(2,1)S(1)}, bf16[1024,512]{0,1:T(8,128)(2,1)S(1)}, bf16[1024,512]{0,1:T(8,128)(2,1)S(1)}) fusion(f32[1024,512]{0,1:T(8,128)} %fusion.26, f32[1024,512]{0,1:T(8,128)} %fusion.27, bf16[1024,3584]{1,0:T(8,128)(2,1)} %bitcast.87, bf16[3584,512]{1,0:T(8,128)(2,1)} %get-tuple-element.16), kind=kOutput, calls=%fused_computation.7 | convolution fusion | flops 3767532544 | bytes 18354176 | tf_op jit(solution)/shard_map/dot_general | solution.py:235
  192.5 8.7 %convolution_convert_fusion = bf16[3584,512]{1,0:T(8,128)(2,1)} fusion(bf16[1024,3584]{1,0:T(8,128)(2,1)} %bitcast.88, bf16[1024,512]{0,1:T(8,128)(2,1)S(1)} %get-tuple-element.30), kind=kOutput, calls=%fused_computation.1 | convolution fusion | flops 3759931392 | bytes 12058624 | tf_op jit(solution)/shard_map/dot_general | solution.py:249
  201.1 5.6 %convolution_convert_fusion.1 = bf16[3584,512]{1,0:T(8,128)(2,1)} fusion(bf16[1024,3584]{1,0:T(8,128)(2,1)S(1)} %bitcast.85, bf16[1024,512]{0,1:T(8,128)(2,1)S(1)} %get-tuple-element.32), kind=kOutput, calls=%fused_computation.2 | convolution fusion | flops 3759931392 | bytes 12058624 | tf_op jit(solution)/shard_map/dot_general | solution.py:249
  206.7 0.0 copy-start.9
  206.7 5.6 %convolution_convert_fusion.2 = bf16[3584,512]{1,0:T(8,128)(2,1)} fusion(bf16[1024,3584]{1,0:T(8,128)(2,1)S(1)} %bitcast.86, bf16[1024,512]{0,1:T(8,128)(2,1)S(1)} %get-tuple-element.31), kind=kOutput, calls=%fused_computation.3 | convolution fusion | flops 3759931392 | bytes 12058624 | tf_op jit(solution)/shard_map/dot_general | solution.py:249
  212.3 0.0 copy-done.9
  212.3 7.4 %fusion.28 = f32[1024,3584]{1,0:T(8,128)} fusion(bf16[1024,512]{0,1:T(8,128)(2,1)S(1)} %get-tuple-element.31, bf16[3584,512]{1,0:T(8,128)(2,1)S(1)} %copy-done.9), kind=kOutput, calls=%fused_computation.50 | convolution fusion | flops 3758096384 | bytes 19398656 | tf_op jit(solution)/shard_map/dot_general | solution.py:243
  219.7 9.3 %add_convert_fusion = bf16[1024,3584]{1,0:T(8,128)(2,1)} fusion(f32[1024,3584]{1,0:T(8,128)} %fusion.28, bf16[1024,512]{0,1:T(8,128)(2,1)S(1)} %get-tuple-element.32, bf16[3584,512]{1,0:T(8,128)(2,1)S(1)} %copy-done.8), kind=kOutput, calls=%fused_computation | convolution fusion | flops 3765436416 | bytes 26738688 | tf_op jit(solution)/shard_map/dot_general | solution.py:244
  229.1 0.1 broadcast_in_dim.65
  229.2 0.2 broadcast_in_dim.66.gates
  229.4 0.0 copy-start.6
  229.4 144.9 %return_rows.1 = (bf16[32,16,3584]{2,1,0:T(8,128)(2,1)}, f32[32,16,128]{2,1,0:T(8,128)S(1)}, bf16[896,1024]{1,0:T(8,128)(2,1)S(1)}, bf16[896,1024]{1,0:T(8,128)(2,1)S(1)}, bf16[896,1024]{1,0:T(8,128)(2,1)}) custom-call(bf16[2,2,16,16,3584]{4,3,2,1,0:T(8,128)(2,1)} %bitcast.62, f32[2,2,16,16,128]{4,3,2,1,0:T(8,128)S(1)} %broadcast_in_dim.66.gates, ...), custom_call_target="tpu_custom_call" | custom-call | tf_op jit(solution)/shard_map/return_rows/pallas_call | solution.py:297
  374.2 0.0 copy-start.2
  374.3 1.2 copy-done.2
  375.5 0.1 copy.35
  375.6 0.0 copy-start.3
  375.6 0.3 select_reduce_fusion.1
  375.8 0.0 copy-done.6
  375.9 0.6 fusion.23
  376.4 4.1 %convolution_convert_fusion.5 = bf16[192,3584]{1,0:T(8,128)(2,1)} fusion(bf16[512,3584]{1,0:T(8,128)(2,1)} %bitcast.66, s32[192]{0:T(256)S(1)} %bitcast.78, s32[192]{0:T(256)S(1)} %bitcast.74), kind=kOutput, calls=%fused_computation.6 | convolution fusion | flops 706117632 | bytes 5047808 | tf_op jit(solution)/shard_map/dot_general | solution.py:249
  380.5 0.0 copy-done.3
  380.5 1.2 copy.41
  381.7 1.2 copy.42
  383.0 0.0 copy-done.4
  383.0 1.2 copy.43
  384.2 0.0 copy-done.1
  (7 shorter events, 0.1 us)
Async XLA Ops:
  0.6 4.2 %copy-start = (bf16[192,3584]{1,0:T(8,128)(2,1)S(1)}, bf16[192,3584]{1,0:T(8,128)(2,1)}, u32[]{:S(2)}) copy-start(bf16[192,3584]{1,0:T(8,128)(2,1)} %param.8) | copy-start | bytes 4128772
  2.6 5.3 %copy-start.5 = (bf16[192,3584]{1,0:T(8,128)(2,1)S(1)}, bf16[192,3584]{1,0:T(8,128)(2,1)}, u32[]{:S(2)}) copy-start(bf16[192,3584]{1,0:T(8,128)(2,1)} %param.7) | copy-start | bytes 4128772
  166.9 9.7 %copy-start.7 = (bf16[2,2,16,16,3584]{4,3,2,1,0:T(8,128)(2,1)S(1)}, bf16[2,2,16,16,3584]{4,3,2,1,0:T(8,128)(2,1)}, u32[]{:S(2)}) copy-start(bf16[2,2,16,16,3584]{4,3,2,1,0:T(8,128)(2,1)} %get-tuple-element.17) | copy-start | bytes 22020100
  166.9 9.7 %copy-start.8 = (bf16[3584,512]{1,0:T(8,128)(2,1)S(1)}, bf16[3584,512]{1,0:T(8,128)(2,1)}, u32[]{:S(2)}) copy-start(bf16[3584,512]{1,0:T(8,128)(2,1)} %get-tuple-element.18) | copy-start | bytes 11010052
  206.7 5.6 %copy-start.9 = (bf16[3584,512]{1,0:T(8,128)(2,1)S(1)}, bf16[3584,512]{1,0:T(8,128)(2,1)}, u32[]{:S(2)}) copy-start(bf16[3584,512]{1,0:T(8,128)(2,1)} %get-tuple-element.19) | copy-start | bytes 11010052
  229.4 146.5 %copy-start.6 = (bf16[192,2]{0,1:T(2,128)(2,1)S(1)}, bf16[192,2]{0,1:T(2,128)(2,1)}, u32[]{:S(2)}) copy-start(bf16[192,2]{0,1:T(2,128)(2,1)} %param.10) | copy-start | bytes 2308
  374.2 1.2 copy-start.2
  375.6 4.9 %copy-start.3 = (bf16[896,1024]{1,0:T(8,128)(2,1)S(1)}, bf16[896,1024]{1,0:T(8,128)(2,1)}, u32[]{:S(2)}) copy-start(bf16[896,1024]{1,0:T(8,128)(2,1)} %copy-done.2) | copy-start | bytes 5505028
  380.5 2.5 copy-start.4
  380.5 3.7 copy-start.1

commit v2 on v1

v2 whole, which is shorter than its diff:
```python
import functools

import jax
import jax.numpy as jnp
from jax import lax
from jax.experimental import pallas as pl
from jax.experimental.pallas import tpu as pltpu
from jax.sharding import PartitionSpec as P

MESH = pl.DeviceIdType.MESH
ROWS = 16


def place():
    ep, plane = lax.axis_index("ep"), lax.axis_index("edp")
    core = lax.rem(ep, 2)
    parity = plane // 2
    beside = plane + 1 - 2 * lax.rem(plane, 2)
    across = 3 - plane
    return ep, ep // 2, core, plane, parity, beside, across


def remote(src, dst, send, recv, ep, plane):
    return pltpu.make_async_remote_copy(
        src_ref=src, dst_ref=dst, send_sem=send, recv_sem=recv,
        device_id=(ep, plane), device_id_type=MESH,
    )


def landed(ref, sem):
    pltpu.make_async_copy(ref, ref, sem).wait()


def layer_kernel(chips, x_send, dy_send, w_gate, w_up, w_down, reply_out, gates_out, g_gate, g_up, g_down,
                 x_all, dy_all, f_gate, f_up, f_down, slope, gated, act, d_gate, d_up, terms, arrived,
                 reply_in, gates_own, gates_in,
                 token_send, token_recv, hand_send, hand_recv, weight_send, weight_recv, relay_send,
                 sum_send, sum_recv, pass_send, pass_recv, out_send, out_recv, back_send, back_recv):
    ep, chip, core, plane, parity, beside, across = place()
    depth, width = w_gate.shape
    half = width // 2
    tile = min(half, 256)
    model_width = 4 * depth
    sibling = ep + 1 - 2 * core
    away = core != parity
    weights = (w_gate, w_up, w_down)
    fulls = (f_gate, f_up, f_down)
    grads = (g_gate, g_up, g_down)
    sends, alls = (x_send, dy_send), (x_all, dy_all)
    f32, bf16 = jnp.float32, jnp.bfloat16

    def rows_of(ref, shard):
        return ref.at[pl.ds(pl.multiple_of(shard * depth, 16), depth)]

    def columns(ref, part):
        return ref.at[:, pl.ds(pl.multiple_of(part * half, 128), half)]

    def block(ref, group, index):
        return ref.at[group, pl.ds(pl.multiple_of(index * ROWS, ROWS), ROWS)]

    for m in range(3):
        @pl.when(away)
        def _(m=m):
            for part in range(2):
                remote(columns(weights[m], part), rows_of(fulls[m], plane), weight_send.at[m, part],
                       weight_recv.at[m, 0], 2 * chip + part, across).start()

    for n in range(2):
        for group in range(2):
            def send(k, carry, n=n, group=group):
                to = lax.rem(chip + k, chips)
                to_plane = plane if group == 0 else across
                kind = parity if group == 0 else 1 - parity
                remote(sends[n].at[2 * to + kind], block(alls[n].at[core], group, chip), token_send.at[n, group],
                       token_recv.at[n, group], 2 * to + core, to_plane).start()
                return carry

            if group == 0:
                pltpu.make_async_copy(sends[n].at[2 * chip + parity], block(alls[n].at[core], 0, chip),
                                      token_recv.at[n, 0]).start()
            lax.fori_loop(1 if group == 0 else 0, chips, send, 0)
        if n == 0:
            for m in range(3):
                @pl.when(jnp.logical_not(away))
                def _(m=m):
                    for part in range(2):
                        remote(columns(weights[m], part), rows_of(fulls[m], plane), weight_send.at[m, part],
                               weight_recv.at[m, 1], 2 * chip + part, beside).start()
                    pltpu.make_async_copy(columns(weights[m], core), rows_of(fulls[m], plane),
                                          weight_recv.at[m, 2]).start()
                    remote(columns(weights[m], 1 - core), rows_of(fulls[m], plane), weight_send.at[m, 2],
                           weight_recv.at[m, 2], sibling, plane).start()

    def relay(m):
        return remote(rows_of(fulls[m], across), rows_of(fulls[m], across), relay_send.at[m],
                      weight_recv.at[m, 3], 2 * chip + core, beside)

    def hand_over(n, group):
        return remote(alls[n].at[core, group], alls[n].at[core, group], hand_send.at[n, group],
                      hand_recv.at[n, group], sibling, plane)

    def pass_on(n, group):
        landed(alls[n].at[core, group], token_recv.at[n, group])
        hand_over(n, group).start()

    def weights_here(m):
        landed(rows_of(fulls[m], beside), weight_recv.at[m, 1])
        landed(rows_of(fulls[m], plane), weight_recv.at[m, 2])
        landed(rows_of(fulls[m], 3 - beside), weight_recv.at[m, 3])

    def product(left, k, group, right, cols):
        deep = min(model_width, 512)
        total = None
        for at in range(0, model_width, deep):
            term = jnp.dot(left[k, group, :, at:at + deep], right[at:at + deep, cols], preferred_element_type=f32)
            total = term if total is None else total + term
        return total

    def tiles(n):
        return pl.ds(pl.multiple_of(n * tile, tile), tile)

    def forward(group):
        def step(i, carry):
            k, cols = i // (half // tile), tiles(lax.rem(i, half // tile))
            pre_gate = product(x_all, k, group, f_gate, cols)
            sigma = jax.nn.sigmoid(pre_gate)
            silu_val = pre_gate * sigma
            gated[k, group, :, cols] = silu_val
            slope[k, group, :, cols] = sigma * (1.0 + pre_gate * (1.0 - sigma))
            pre_up = product(x_all, k, group, f_up, cols)
            act[k, group, :, cols] = (gated[k, group, :, cols] * pre_up).astype(bf16)
            slope[k, group, :, cols] = slope[k, group, :, cols] * pre_up
            return carry

        lax.fori_loop(0, 2 * (half // tile), step, 0)

    def backward(k, group):
        gates_own[k, group] = jnp.zeros(gates_own.shape[2:], f32)

        def step(n, carry):
            cols = tiles(n)
            back = product(dy_all, k, group, f_down, cols)
            d_gate[k, group, :, cols] = (back * slope[k, group, :, cols]).astype(bf16)
            d_up[k, group, :, cols] = (back * gated[k, group, :, cols]).astype(bf16)
            part = jnp.sum(act[k, group, :, cols].astype(f32) * back, axis=1, keepdims=True)
            gates_own[k, group] = gates_own[k, group] + part
            return carry

        lax.fori_loop(0, half // tile, step, 0)

    relay_order = (0, 1)
    for m in relay_order:
        landed(rows_of(fulls[m], across), weight_recv.at[m, 0])
        relay(m).start()
    pass_on(0, 0)
    landed(rows_of(f_down, across), weight_recv.at[2, 0])
    relay(2).start()
    pass_on(0, 1)
    pass_on(1, 0)
    weights_here(0)
    weights_here(1)
    for group in range(2):
        landed(x_all.at[1 - core, group], hand_recv.at[0, group])
        forward(group)
    weights_here(2)
    backward(core, 0)
    landed(dy_all.at[1 - core, 0], hand_recv.at[1, 0])
    backward(1 - core, 0)
    pass_on(1, 1)
    backward(core, 1)
    landed(dy_all.at[1 - core, 1], hand_recv.at[1, 1])
    backward(1 - core, 1)

    def moved(m, i):
        return remote(terms.at[m, i], arrived.at[m, i], sum_send.at[m, i], sum_recv.at[m, i],
                      2 * chip + core, beside)

    def gradients(i, carry):
        shard = jnp.where(i == 0, 3 - beside, jnp.where(i == 1, beside, jnp.where(i == 2, across, plane)))
        cols = pl.ds(pl.multiple_of(shard * depth, 128), depth)
        over = (((0,), (0,)), ((), ()))

        def accumulate(m, left, right):
            def step(n, carry):
                total = None
                for k in range(2):
                    for group in range(2):
                        term = lax.dot_general(left[k, group, :, cols], right[k, group, :, tiles(n)], over,
                                               preferred_element_type=f32)
                        total = term if total is None else total + term
                terms[m, i, :, tiles(n)] = total.astype(bf16)
                return carry

            lax.fori_loop(0, half // tile, step, 0)

            @pl.when(i < 2)
            def _():
                moved(m, i).start()

        accumulate(0, x_all, d_gate)
        accumulate(1, x_all, d_up)
        accumulate(2, dy_all, act)
        return carry

    lax.fori_loop(0, 4, gradients, 0)

    for n in range(2):
        for group in range(2):
            hand_over(n, group).wait_send()

    def replies(k, group, other):
        wide = min(model_width, 512)

        def step(n, carry):
            cols = pl.ds(pl.multiple_of(n * wide, wide), wide)
            contract = (((1,), (1,)), ((), ()))
            total = lax.dot_general(d_gate[k, group], f_gate[cols], contract, preferred_element_type=f32)
            total = total + lax.dot_general(d_up[k, group], f_up[cols], contract, preferred_element_type=f32)
            if other is not None:
                total = total + other[group, :, cols].astype(f32)
            x_all[k, group, :, cols] = total.astype(bf16)
            return carry

        lax.fori_loop(0, model_width // wide, step, 0)

    gates_pass = remote(gates_own.at[1 - core], gates_in, pass_send.at[2], pass_recv.at[2], sibling, plane)
    gates_pass.start()

    def reply_pass(group):
        return remote(x_all.at[1 - core, group], reply_in.at[group], pass_send.at[group], pass_recv.at[group],
                      sibling, plane)

    for group in (1, 0):
        replies(1 - core, group, None)
        reply_pass(group).start()
    gates_pass.wait()
    gates_own[core] = gates_own[core] + gates_in[...]
    for group in (1, 0):
        reply_pass(group).wait()
        replies(core, group, reply_in)

        def send(k, carry, group=group):
            to = lax.rem(chip + k, chips)
            to_plane = plane if group == 0 else across
            remote(block(x_all.at[core], group, to), reply_out.at[2 * chip + parity], back_send.at[0, group],
                   back_recv.at[0, group], 2 * to + core, to_plane).start()
            remote(block(gates_own.at[core], group, to), gates_out.at[2 * chip + parity], back_send.at[1, group],
                   back_recv.at[1, group], 2 * to + core, to_plane).start()
            return carry

        if group == 0:
            pltpu.make_async_copy(block(x_all.at[core], 0, chip), reply_out.at[2 * chip + parity],
                                  back_recv.at[0, 0]).start()
            pltpu.make_async_copy(block(gates_own.at[core], 0, chip), gates_out.at[2 * chip + parity],
                                  back_recv.at[1, 0]).start()
        lax.fori_loop(1 if group == 0 else 0, chips, send, 0)

    for i in range(2):
        for m in range(3):
            moved(m, i).wait()
            step = 128

            def add(k, carry, m=m, i=i):
                rows = pl.ds(pl.multiple_of(k * step, step), step)
                total = terms[m, 2 + i, rows].astype(f32) + arrived[m, i, rows].astype(f32)
                terms[m, 2 + i, rows] = total.astype(bf16)
                return carry

            lax.fori_loop(0, depth // step, add, 0)
            if i == 0:
                remote(terms.at[m, 2], columns(grads[m], core), out_send.at[m, 0], out_recv.at[m, core],
                       2 * chip + parity, across).start()
            else:
                @pl.when(core == parity)
                def _(m=m):
                    pltpu.make_async_copy(terms.at[m, 3], columns(grads[m], core), out_recv.at[m, core]).start()

                @pl.when(core != parity)
                def _(m=m):
                    remote(terms.at[m, 3], columns(grads[m], core), out_send.at[m, 1], out_recv.at[m, core],
                           2 * chip + parity, plane).start()

    for m in range(3):
        relay(m).wait_send()
        for part in range(2):
            landed(columns(weights[m], part), weight_send.at[m, part])

        @pl.when(jnp.logical_not(away))
        def _(m=m):
            landed(columns(weights[m], 0), weight_send.at[m, 2])
        landed(terms.at[m, 2], out_send.at[m, 0])

        @pl.when(core != parity)
        def _(m=m):
            landed(terms.at[m, 3], out_send.at[m, 1])
        for part in range(2):
            landed(columns(grads[m], part), out_recv.at[m, part])
    sent = pl.ds(0, (chips - 1) * ROWS)
    for n in range(2):
        landed(alls[n].at[core, 0, sent], token_send.at[n, 0])
        landed(alls[n].at[core, 1], token_send.at[n, 1])
    for n, own in enumerate((x_all, gates_own)):
        landed(own.at[core, 0, sent], back_send.at[n, 0])
        landed(own.at[core, 1], back_send.at[n, 1])
        for group in range(2):
            landed(own.at[core, group], back_recv.at[n, group])


def over_rows(left, right):
    return lax.dot_general(left, right, (((0,), (0,)), ((), ())), preferred_element_type=jnp.float32)


def shards(tokens, upstream, expert_ids, gate_values, w_gate, w_up, w_down):
    experts = lax.axis_size("ep")
    chips = experts // 2
    tok_count, top_count = expert_ids.shape
    model_width = tokens.shape[1]
    depth, width = w_gate.shape[1:]
    half = width // 2
    buffer_rows = experts * ROWS
    bf16 = jnp.bfloat16
    flat_ids = expert_ids.reshape(-1)
    onehot = (flat_ids[:, None] == jnp.arange(experts, dtype=jnp.int32)[None, :]).astype(jnp.int32)
    slot_idx = jnp.sum(jnp.cumsum(onehot, axis=0) * onehot, axis=1) - 1
    target = (flat_ids * ROWS + slot_idx).reshape(tok_count, top_count)
    slots = jnp.arange(buffer_rows, dtype=jnp.int32)
    picks = [slots[:, None] == target[None, :, k] for k in range(top_count)]
    zero = jnp.zeros((), bf16)
    dispatch_map = sum(pick.astype(bf16) for pick in picks)
    scaled_map = sum(jnp.where(pick, gate_values[None, :, k], zero) for k, pick in enumerate(picks))
    x_send = jnp.dot(dispatch_map, tokens, preferred_element_type=jnp.float32).astype(bf16)
    dy_send = jnp.dot(scaled_map, upstream, preferred_element_type=jnp.float32).astype(bf16)

    anywhere = pl.BlockSpec(memory_space=pl.ANY)
    dma = pltpu.SemaphoreType.DMA
    tall = chips * ROWS
    rows_buffer = pltpu.VMEM((2, 2, tall, model_width), bf16)
    full_buffer = pltpu.VMEM((4 * depth, half), bf16)
    wide_buffer = pltpu.VMEM((2, 2, tall, half), jnp.float32)
    narrow_buffer = pltpu.VMEM((2, 2, tall, half), bf16)
    grad_shape = jax.ShapeDtypeStruct((depth, width), bf16)
    reply_out, gates_out, g_gate, g_up, g_down = pl.pallas_call(
        functools.partial(layer_kernel, chips),
        out_shape=[jax.ShapeDtypeStruct((experts, ROWS, model_width), bf16),
                   jax.ShapeDtypeStruct((experts, ROWS, 128), jnp.float32)] + [grad_shape] * 3,
        in_specs=[anywhere] * 5,
        out_specs=[anywhere] * 5,
        scratch_shapes=[
            rows_buffer, rows_buffer, full_buffer, full_buffer, full_buffer,
            wide_buffer, wide_buffer, narrow_buffer, narrow_buffer, narrow_buffer,
            pltpu.VMEM((3, 4, depth, half), bf16), pltpu.VMEM((3, 2, depth, half), bf16),
            pltpu.VMEM((2, tall, model_width), bf16),
            pltpu.VMEM((2, 2, tall, 128), jnp.float32), pltpu.VMEM((2, tall, 128), jnp.float32),
            dma((2, 2)), dma((2, 2)), dma((2, 2)), dma((2, 2)), dma((3, 3)), dma((3, 4)), dma((3,)),
            dma((3, 2)), dma((3, 2)), dma((3,)), dma((3,)), dma((3, 2)), dma((3, 2)), dma((2, 2)), dma((2, 2))],
        compiler_params=pltpu.CompilerParams(has_side_effects=True, vmem_limit_bytes=60 << 20),
        name="expert_layer",
    )(x_send.reshape(experts, ROWS, model_width), dy_send.reshape(experts, ROWS, model_width),
      w_gate[0], w_up[0], w_down[0])

    token_grad = over_rows(dispatch_map, reply_out.reshape(buffer_rows, model_width)).astype(bf16)
    gate_rows = gates_out.reshape(buffer_rows, 128)[:, 0]
    gate_grad = jnp.stack([jnp.sum(jnp.where(pick, gate_rows[:, None], 0.0), axis=0) for pick in picks], axis=1)
    gate_grad = (gate_grad / gate_values.astype(jnp.float32)).astype(bf16)
    return token_grad, gate_grad, g_gate[None], g_up[None], g_down[None]


def solution(mesh):
    tokens_spec, weights_spec = P(("ep", "edp"), None), P("ep", "edp", None)
    return jax.shard_map(
        shards, mesh=mesh,
        in_specs=(tokens_spec,) * 4 + (weights_spec,) * 3,
        out_specs=(tokens_spec,) * 2 + (weights_spec,) * 3,
        check_vma=False,
    )
```

time: 391 us -> 338 us (0.86)
  the two profiles are of different devices: /device:TPU:112 before, /device:TPU:18 now
where the time goes in v2:
time: 338 us
  Pallas kernels  316 us (93%)
  matrix products  10.4 us (3%)
  local copies, waits for them, and re-layouts  8.03 us (2%)
    pallas_call x1, Pallas kernels, shards(): pl.pallas_call(functools.partial(layer_kernel, chips), out_shape=[jax.Sha...  316 us

profile of v2, /device:TPU:18, one launch (start us, length us, event | category | flops | bytes accessed | tf_op | source)
XLA Modules:
  0.0 337.8 jit_solution(10420640729874328626)
XLA Ops:
  0.6 0.0 copy-start
  0.6 0.8 slice_reduce_fusion.2
  1.5 0.8 copy.30
  2.3 0.1 eq.60
  2.4 0.1 eq.56
  2.6 0.9 reduce-window.6
  3.5 0.2 slice_reduce_fusion
  3.7 0.1 fusion.20
  3.8 0.1 sub.7
  4.0 0.1 copy.33
  4.1 0.7 multiply_add_fusion
  4.8 0.0 copy-done
  4.8 0.0 copy-start.4
  4.8 3.1 convolution_convert_fusion
  7.9 0.0 copy-done.4
  7.9 3.1 convolution_convert_fusion.1
  11.0 316.1 %expert_layer.1 = (bf16[32,16,3584]{2,1,0:T(8,128)(2,1)}, f32[32,16,128]{2,1,0:T(8,128)}, bf16[896,1024]{1,0:T(8,128)(2,1)}, bf16[896,1024]{1,0:T(8,128)(2,1)}, bf16[896,1024]{1,0:T(8,128)(2,1)}) custom-call(bf16[32,16,3584]{2,1,0:T(8,128)(2,1)} %bitcast.36, bf16[32,16,3584]{2,1,0:T(8,128)(2,1)} %bitcast.35, bf16[896,1024]{1,0:T(8,128)(2,1)} %bitcast.38, ...), custom_call_target="tpu_custom_call" | custom-call | tf_op jit(solution)/shard_map/expert_layer/pallas_call | solution.py:342
  327.0 0.0 copy-start.5
  327.0 0.0 copy-start.6
  327.1 0.0 copy-start.3
  327.1 4.2 %convolution_convert_fusion.2 = bf16[192,3584]{1,0:T(8,128)(2,1)} fusion(bf16[512,3584]{1,0:T(8,128)(2,1)} %bitcast.37, s32[192]{0:T(256)S(1)} %bitcast.51, s32[192]{0:T(256)S(1)} %bitcast.47), kind=kOutput, calls=%fused_computation.2 | convolution fusion | flops 706117632 | bytes 5047808 | tf_op jit(solution)/shard_map/dot_general | solution.py:310
  331.3 0.0 copy-done.5
  331.3 0.1 copy.35
  331.4 0.3 select_reduce_fusion.1
  331.7 0.0 copy-done.6
  331.7 0.6 fusion.22
  332.2 0.0 copy-done.3
  332.2 0.0 copy-start.2
  332.2 1.2 copy.41
  333.5 0.9 copy-done.2
  334.4 0.0 copy-start.1
  334.4 1.2 copy.42
  335.6 0.9 copy-done.1
  336.6 1.2 copy.43
  (4 shorter events, 0.1 us)
Async XLA Ops:
  0.6 4.1 %copy-start = (bf16[192,3584]{1,0:T(8,128)(2,1)S(1)}, bf16[192,3584]{1,0:T(8,128)(2,1)}, u32[]{:S(2)}) copy-start(bf16[192,3584]{1,0:T(8,128)(2,1)} %param.8) | copy-start | bytes 4128772
  4.8 3.1 copy-start.4
  327.0 4.3 %copy-start.5 = (f32[32,16,128]{2,1,0:T(8,128)S(1)}, f32[32,16,128]{2,1,0:T(8,128)}, u32[]{:S(2)}) copy-start(f32[32,16,128]{2,1,0:T(8,128)} %get-tuple-element.11) | copy-start | bytes 786436
  327.0 4.6 %copy-start.6 = (bf16[192,2]{0,1:T(2,128)(2,1)S(1)}, bf16[192,2]{0,1:T(2,128)(2,1)}, u32[]{:S(2)}) copy-start(bf16[192,2]{0,1:T(2,128)(2,1)} %param.10) | copy-start | bytes 2308
  327.1 5.2 %copy-start.3 = (bf16[896,1024]{1,0:T(8,128)(2,1)S(1)}, bf16[896,1024]{1,0:T(8,128)(2,1)}, u32[]{:S(2)}) copy-start(bf16[896,1024]{1,0:T(8,128)(2,1)} %get-tuple-element.12) | copy-start | bytes 5505028
  332.2 2.2 copy-start.2
  334.4 2.2 copy-start.1

commit v3 on v2

--- a/solution.py
+++ b/solution.py
@@ -31,22 +31,27 @@
     pltpu.make_async_copy(ref, ref, sem).wait()
 
 
-def layer_kernel(chips, x_send, dy_send, w_gate, w_up, w_down, reply_out, gates_out, g_gate, g_up, g_down,
+def layer_kernel(chips, tokens, upstream, info_own, w_gate, w_up, w_down,
+                 mix_own, mix_across, gates_out, gates_across, g_gate, g_up, g_down,
                  x_all, dy_all, f_gate, f_up, f_down, slope, gated, act, d_gate, d_up, terms, arrived,
-                 reply_in, gates_own, gates_in,
+                 x_stage, dy_stage, gates_own, gates_in, gates_back, gates_mix, info_in,
+                 load_sem, swap_send, swap_recv, info_sem, stay_sem,
                  token_send, token_recv, hand_send, hand_recv, weight_send, weight_recv, relay_send,
-                 sum_send, sum_recv, pass_send, pass_recv, out_send, out_recv, back_send, back_recv):
+                 sum_send, sum_recv, pass_send, pass_recv, out_send, out_recv, back_send, back_recv,
+                 mix_send, mix_recv):
     ep, chip, core, plane, parity, beside, across = place()
     depth, width = w_gate.shape
     half = width // 2
     tile = min(half, 256)
-    model_width = 4 * depth
+    tok_count, model_width = tokens.shape
+    tall = chips * ROWS
     sibling = ep + 1 - 2 * core
     away = core != parity
     weights = (w_gate, w_up, w_down)
     fulls = (f_gate, f_up, f_down)
     grads = (g_gate, g_up, g_down)
-    sends, alls = (x_send, dy_send), (x_all, dy_all)
+    stages, alls = (x_stage, dy_stage), (x_all, dy_all)
+    reply_back, reply_in = x_stage, dy_stage
     f32, bf16 = jnp.float32, jnp.bfloat16
 
     def rows_of(ref, shard):
@@ -58,38 +63,114 @@
     def block(ref, group, index):
         return ref.at[group, pl.ds(pl.multiple_of(index * ROWS, ROWS), ROWS)]
 
-    for m in range(3):
+    chunks = model_width // half
+    fit = depth // tok_count
+    slabs = -(-chunks // fit)
+
+    def chunk_of(n, group, j):
+        slab = slabs * (2 * n + group) + j // fit
+        return terms.at[slab // 4, slab % 4, pl.ds(j % fit * tok_count, tok_count)]
+
+    def source_of(n, j):
+        return (tokens, upstream)[n].at[:, pl.ds(j * half, half)]
+
+    def loads(n):
+        return [pltpu.make_async_copy(source_of(n, j), chunk_of(n, 0, j), load_sem.at[n, j]) for j in range(chunks)]
+
+    def swaps(n):
+        return [remote(source_of(n, j), chunk_of(n, 1, j), swap_send.at[n, j], swap_recv.at[n, j], ep, across)
+                for j in range(chunks)]
+
+    def info_swap():
+        return remote(info_own, info_in, info_sem.at[0], info_sem.at[1], ep, across)
+
+    def hits(group):
+        info = info_own if group == 0 else info_in
+        rows = lax.broadcasted_iota(jnp.int32, (tall, tok_count), 0)
+        slot = (rows + (rows // ROWS + parity) * ROWS).astype(f32)
+        return [slot == info[k:k + 1, :tok_count] for k in range(2)]
+
+    def picks(n, group):
+        info = info_own if group == 0 else info_in
+        levels = [info[2 + k:3 + k, :tok_count] if n else jnp.ones((1, tok_count), f32) for k in range(2)]
+        terms_of = [jnp.where(hit, level, 0.0) for hit, level in zip(hits(group), levels)]
+        return (terms_of[0] + terms_of[1]).astype(bf16)
+
+    def dispatch(n, group):
+        chosen = picks(n, group)
+        for j in range(chunks):
+            rows = jnp.dot(chosen, chunk_of(n, group, j)[...], preferred_element_type=f32)
+            stages[n][group, :, j * half:(j + 1) * half] = rows.astype(bf16)
+
+    def stays(n, group):
+        return pltpu.make_async_copy(block(stages[n], group, chip), block(alls[n].at[core], group, chip),
+                                     stay_sem.at[n, group])
+
+    def spread(n, group):
+        def send(k, carry):
+            to = lax.rem(chip + k, chips)
+            remote(block(stages[n], group, to), block(alls[n].at[core], group, chip), token_send.at[n, group],
+                   token_recv.at[n, group], 2 * to + core, plane).start()
+            return carry
+
+        stays(n, group).start()
+        lax.fori_loop(1, chips, send, 0)
+
+    def spread_done(n, group):
+        stays(n, group).wait()
+        landed(stages[n].at[group, pl.ds(0, (chips - 1) * ROWS)], token_send.at[n, group])
+
+    def away_weights(m):
         @pl.when(away)
-        def _(m=m):
+        def _():
             for part in range(2):
                 remote(columns(weights[m], part), rows_of(fulls[m], plane), weight_send.at[m, part],
                        weight_recv.at[m, 0], 2 * chip + part, across).start()
 
+    def home_weights(m):
+        @pl.when(jnp.logical_not(away))
+        def _():
+            for part in range(2):
+                remote(columns(weights[m], part), rows_of(fulls[m], plane), weight_send.at[m, part],
+                       weight_recv.at[m, 1], 2 * chip + part, beside).start()
+            pltpu.make_async_copy(columns(weights[m], core), rows_of(fulls[m], plane),
+                                  weight_recv.at[m, 2]).start()
+            remote(columns(weights[m], 1 - core), rows_of(fulls[m], plane), weight_send.at[m, 2],
+                   weight_recv.at[m, 2], sibling, plane).start()
+
     for n in range(2):
-        for group in range(2):
-            def send(k, carry, n=n, group=group):
-                to = lax.rem(chip + k, chips)
-                to_plane = plane if group == 0 else across
-                kind = parity if group == 0 else 1 - parity
-                remote(sends[n].at[2 * to + kind], block(alls[n].at[core], group, chip), token_send.at[n, group],
-                       token_recv.at[n, group], 2 * to + core, to_plane).start()
-                return carry
-
-            if group == 0:
-                pltpu.make_async_copy(sends[n].at[2 * chip + parity], block(alls[n].at[core], 0, chip),
-                                      token_recv.at[n, 0]).start()
-            lax.fori_loop(1 if group == 0 else 0, chips, send, 0)
-        if n == 0:
-            for m in range(3):
-                @pl.when(jnp.logical_not(away))
-                def _(m=m):
-                    for part in range(2):
-                        remote(columns(weights[m], part), rows_of(fulls[m], plane), weight_send.at[m, part],
-                               weight_recv.at[m, 1], 2 * chip + part, beside).start()
-                    pltpu.make_async_copy(columns(weights[m], core), rows_of(fulls[m], plane),
-                                          weight_recv.at[m, 2]).start()
-                    remote(columns(weights[m], 1 - core), rows_of(fulls[m], plane), weight_send.at[m, 2],
-                           weight_recv.at[m, 2], sibling, plane).start()
+        for copy in loads(n):
+            copy.start()
+    barrier = pltpu.get_barrier_semaphore()
+
+    def greet(k, carry):
+        pl.semaphore_signal(barrier, inc=1, device_id=(2 * lax.rem(chip + k, chips) + core, plane),
+                            device_id_type=MESH)
+        return carry
+
+    lax.fori_loop(1, chips, greet, 0)
+    for other in ((sibling, plane), (ep, across), (sibling, across), (ep, beside), (sibling, beside)):
+        pl.semaphore_signal(barrier, inc=1, device_id=other, device_id_type=MESH)
+    for copy in loads(0):
+        copy.wait()
+    dispatch(0, 0)
+    pl.semaphore_wait(barrier, chips + 4)
+
+    info_swap().start()
+    for copy in swaps(0):
+        copy.start()
+    away_weights(0)
+    for m in range(3):
+        home_weights(m)
+    for copy in swaps(1):
+        copy.start()
+    away_weights(1)
+    away_weights(2)
+    spread(0, 0)
+    for copy in loads(1):
+        copy.wait()
+    dispatch(1, 0)
+    spread(1, 0)
 
     def relay(m):
         return remote(rows_of(fulls[m], across), rows_of(fulls[m], across), relay_send.at[m],
@@ -100,7 +181,8 @@
                       hand_recv.at[n, group], sibling, plane)
 
     def pass_on(n, group):
-        landed(alls[n].at[core, group], token_recv.at[n, group])
+        landed(alls[n].at[core, group, pl.ds(0, (chips - 1) * ROWS)], token_recv.at[n, group])
+        spread_done(n, group)
         hand_over(n, group).start()
 
     def weights_here(m):
@@ -148,28 +230,37 @@
 
         lax.fori_loop(0, half // tile, step, 0)
 
-    relay_order = (0, 1)
-    for m in relay_order:
+    def start_relay(m):
         landed(rows_of(fulls[m], across), weight_recv.at[m, 0])
         relay(m).start()
+
+    info_swap().wait()
+    for copy in swaps(0):
+        copy.wait_recv()
+    dispatch(0, 1)
+    spread(0, 1)
+    start_relay(0)
     pass_on(0, 0)
-    landed(rows_of(f_down, across), weight_recv.at[2, 0])
-    relay(2).start()
+    for copy in swaps(1):
+        copy.wait_recv()
+    dispatch(1, 1)
     pass_on(0, 1)
+    spread(1, 1)
     pass_on(1, 0)
+    start_relay(1)
+    pass_on(1, 1)
     weights_here(0)
     weights_here(1)
+    landed(x_all.at[1 - core, 0], hand_recv.at[0, 0])
+    forward(0)
+    start_relay(2)
+    landed(x_all.at[1 - core, 1], hand_recv.at[0, 1])
+    forward(1)
+    weights_here(2)
     for group in range(2):
-        landed(x_all.at[1 - core, group], hand_recv.at[0, group])
-        forward(group)
-    weights_here(2)
-    backward(core, 0)
-    landed(dy_all.at[1 - core, 0], hand_recv.at[1, 0])
-    backward(1 - core, 0)
-    pass_on(1, 1)
-    backward(core, 1)
-    landed(dy_all.at[1 - core, 1], hand_recv.at[1, 1])
-    backward(1 - core, 1)
+        landed(dy_all.at[1 - core, group], hand_recv.at[1, group])
+        backward(core, group)
+        backward(1 - core, group)
 
     def moved(m, i):
         return remote(terms.at[m, i], arrived.at[m, i], sum_send.at[m, i], sum_recv.at[m, i],
@@ -241,21 +332,44 @@
 
         def send(k, carry, group=group):
             to = lax.rem(chip + k, chips)
-            to_plane = plane if group == 0 else across
-            remote(block(x_all.at[core], group, to), reply_out.at[2 * chip + parity], back_send.at[0, group],
-                   back_recv.at[0, group], 2 * to + core, to_plane).start()
-            remote(block(gates_own.at[core], group, to), gates_out.at[2 * chip + parity], back_send.at[1, group],
-                   back_recv.at[1, group], 2 * to + core, to_plane).start()
+            for n, (own, back) in enumerate(((x_all, reply_back), (gates_own, gates_back))):
+                remote(block(own.at[core], group, to), block(back, group, chip), back_send.at[n, group],
+                       back_recv.at[n, group], 2 * to + core, plane).start()
             return carry
 
+        for n, (own, back) in enumerate(((x_all, reply_back), (gates_own, gates_back))):
+            pltpu.make_async_copy(block(own.at[core], group, chip), block(back, group, chip),
+                                  back_recv.at[n, group]).start()
+        lax.fori_loop(1, chips, send, 0)
+
+    def combine(group):
+        landed(reply_back.at[group], back_recv.at[0, group])
+        landed(gates_back.at[group], back_recv.at[1, group])
+        chosen = picks(0, group)
+        for j in range(chunks):
+            cols = slice(j * half, (j + 1) * half)
+            total = lax.dot_general(chosen, reply_back[group, :, cols], (((0,), (0,)), ((), ())),
+                                    preferred_element_type=f32)
+            dy_all[0, group, 0:tok_count, cols] = total.astype(bf16)
+        gates_mix[group] = jnp.zeros(gates_mix.shape[1:], f32)
+        for k, hit in enumerate(hits(group)):
+            values = jnp.where(hit, gates_back[group, :, 0:1], 0.0)
+            gates_mix[group, k:k + 1, 0:tok_count] = jnp.sum(values, axis=0, keepdims=True)
+
+    def mixed(group):
+        rows = dy_all.at[0, group, pl.ds(0, tok_count)]
         if group == 0:
-            pltpu.make_async_copy(block(x_all.at[core], 0, chip), reply_out.at[2 * chip + parity],
-                                  back_recv.at[0, 0]).start()
-            pltpu.make_async_copy(block(gates_own.at[core], 0, chip), gates_out.at[2 * chip + parity],
-                                  back_recv.at[1, 0]).start()
-        lax.fori_loop(1 if group == 0 else 0, chips, send, 0)
+            return [pltpu.make_async_copy(rows, mix_own, mix_send.at[0, 0]),
+                    pltpu.make_async_copy(gates_mix.at[0], gates_out, mix_send.at[0, 1])]
+        return [remote(rows, mix_across, mix_send.at[1, 0], mix_recv.at[0], ep, across),
+                remote(gates_mix.at[1], gates_across, mix_send.at[1, 1], mix_recv.at[1], ep, across)]
 
     for i in range(2):
+        if i == 1:
+            for group in (1, 0):
+                combine(group)
+                for copy in mixed(group):
+                    copy.start()
         for m in range(3):
             moved(m, i).wait()
             step = 128
@@ -295,19 +409,15 @@
             landed(terms.at[m, 3], out_send.at[m, 1])
         for part in range(2):
             landed(columns(grads[m], part), out_recv.at[m, part])
-    sent = pl.ds(0, (chips - 1) * ROWS)
     for n in range(2):
-        landed(alls[n].at[core, 0, sent], token_send.at[n, 0])
-        landed(alls[n].at[core, 1], token_send.at[n, 1])
+        for copy in swaps(n):
+            copy.wait_send()
     for n, own in enumerate((x_all, gates_own)):
-        landed(own.at[core, 0, sent], back_send.at[n, 0])
-        landed(own.at[core, 1], back_send.at[n, 1])
         for group in range(2):
-            landed(own.at[core, group], back_recv.at[n, group])
-
-
-def over_rows(left, right):
-    return lax.dot_general(left, right, (((0,), (0,)), ((), ())), preferred_element_type=jnp.float32)
+            landed(own.at[core, group, pl.ds(0, (chips - 1) * ROWS)], back_send.at[n, group])
+    for group in range(2):
+        for copy in mixed(group):
+            copy.wait()
 
 
 def shards(tokens, upstream, expert_ids, gate_values, w_gate, w_up, w_down):
@@ -317,19 +427,14 @@
     model_width = tokens.shape[1]
     depth, width = w_gate.shape[1:]
     half = width // 2
-    buffer_rows = experts * ROWS
     bf16 = jnp.bfloat16
     flat_ids = expert_ids.reshape(-1)
     onehot = (flat_ids[:, None] == jnp.arange(experts, dtype=jnp.int32)[None, :]).astype(jnp.int32)
     slot_idx = jnp.sum(jnp.cumsum(onehot, axis=0) * onehot, axis=1) - 1
     target = (flat_ids * ROWS + slot_idx).reshape(tok_count, top_count)
-    slots = jnp.arange(buffer_rows, dtype=jnp.int32)
-    picks = [slots[:, None] == target[None, :, k] for k in range(top_count)]
-    zero = jnp.zeros((), bf16)
-    dispatch_map = sum(pick.astype(bf16) for pick in picks)
-    scaled_map = sum(jnp.where(pick, gate_values[None, :, k], zero) for k, pick in enumerate(picks))
-    x_send = jnp.dot(dispatch_map, tokens, preferred_element_type=jnp.float32).astype(bf16)
-    dy_send = jnp.dot(scaled_map, upstream, preferred_element_type=jnp.float32).astype(bf16)
+    lines = jnp.concatenate([target.astype(jnp.float32), gate_values.astype(jnp.float32)], axis=1)
+    lanes = -(-tok_count // 128) * 128
+    info = jnp.pad(lines.T, ((0, 4), (0, lanes - tok_count)))
 
     anywhere = pl.BlockSpec(memory_space=pl.ANY)
     dma = pltpu.SemaphoreType.DMA
@@ -339,28 +444,32 @@
     wide_buffer = pltpu.VMEM((2, 2, tall, half), jnp.float32)
     narrow_buffer = pltpu.VMEM((2, 2, tall, half), bf16)
     grad_shape = jax.ShapeDtypeStruct((depth, width), bf16)
-    reply_out, gates_out, g_gate, g_up, g_down = pl.pallas_call(
+    mix_shape = jax.ShapeDtypeStruct((tok_count, model_width), bf16)
+    info_shape = jax.ShapeDtypeStruct(info.shape, jnp.float32)
+    mix_own, mix_across, gates_own, gates_across, g_gate, g_up, g_down = pl.pallas_call(
         functools.partial(layer_kernel, chips),
-        out_shape=[jax.ShapeDtypeStruct((experts, ROWS, model_width), bf16),
-                   jax.ShapeDtypeStruct((experts, ROWS, 128), jnp.float32)] + [grad_shape] * 3,
-        in_specs=[anywhere] * 5,
-        out_specs=[anywhere] * 5,
+        out_shape=[mix_shape] * 2 + [info_shape] * 2 + [grad_shape] * 3,
+        in_specs=[anywhere] * 2 + [pl.BlockSpec(memory_space=pltpu.VMEM)] + [anywhere] * 3,
+        out_specs=[anywhere] * 7,
         scratch_shapes=[
             rows_buffer, rows_buffer, full_buffer, full_buffer, full_buffer,
             wide_buffer, wide_buffer, narrow_buffer, narrow_buffer, narrow_buffer,
             pltpu.VMEM((3, 4, depth, half), bf16), pltpu.VMEM((3, 2, depth, half), bf16),
-            pltpu.VMEM((2, tall, model_width), bf16),
+            pltpu.VMEM((2, tall, model_width), bf16), pltpu.VMEM((2, tall, model_width), bf16),
             pltpu.VMEM((2, 2, tall, 128), jnp.float32), pltpu.VMEM((2, tall, 128), jnp.float32),
+            pltpu.VMEM((2, tall, 128), jnp.float32), pltpu.VMEM((2, 8, lanes), jnp.float32),
+            pltpu.VMEM((8, lanes), jnp.float32),
+            dma((2, model_width // half)), dma((2, model_width // half)), dma((2, model_width // half)),
+            dma((2,)), dma((2, 2)),
             dma((2, 2)), dma((2, 2)), dma((2, 2)), dma((2, 2)), dma((3, 3)), dma((3, 4)), dma((3,)),
-            dma((3, 2)), dma((3, 2)), dma((3,)), dma((3,)), dma((3, 2)), dma((3, 2)), dma((2, 2)), dma((2, 2))],
-        compiler_params=pltpu.CompilerParams(has_side_effects=True, vmem_limit_bytes=60 << 20),
+            dma((3, 2)), dma((3, 2)), dma((3,)), dma((3,)), dma((3, 2)), dma((3, 2)), dma((2, 2)), dma((2, 2)),
+            dma((2, 2)), dma((2,))],
+        compiler_params=pltpu.CompilerParams(has_side_effects=True, collective_id=0, vmem_limit_bytes=60 << 20),
         name="expert_layer",
-    )(x_send.reshape(experts, ROWS, model_width), dy_send.reshape(experts, ROWS, model_width),
-      w_gate[0], w_up[0], w_down[0])
-
-    token_grad = over_rows(dispatch_map, reply_out.reshape(buffer_rows, model_width)).astype(bf16)
-    gate_rows = gates_out.reshape(buffer_rows, 128)[:, 0]
-    gate_grad = jnp.stack([jnp.sum(jnp.where(pick, gate_rows[:, None], 0.0), axis=0) for pick in picks], axis=1)
+    )(tokens, upstream, info, w_gate[0], w_up[0], w_down[0])
+
+    token_grad = (mix_own.astype(jnp.float32) + mix_across.astype(jnp.float32)).astype(bf16)
+    gate_grad = (gates_own + gates_across)[:top_count, :tok_count].T
     gate_grad = (gate_grad / gate_values.astype(jnp.float32)).astype(bf16)
     return token_grad, gate_grad, g_gate[None], g_up[None], g_down[None]
 

time: 338 us -> 291 us (0.86)
  the two profiles are of different devices: /device:TPU:18 before, /device:TPU:112 now
where the time goes in v3:
time: 291 us; the launch traced here: 290 us
  Pallas kernels  275 us (95%)
  local copies, waits for them, and re-layouts  7.68 us (3%)
  other arithmetic  6.99 us (2%)
    pallas_call x1, Pallas kernels, shards(): pl.pallas_call(functools.partial(layer_kernel, chips), out_shape=[mix_sha...  275 us
    unnamed x12, local copies, waits for them, and re-layouts  6.35 us

profile of v3, /device:TPU:112, one launch (start us, length us, event | category | flops | bytes accessed | tf_op | source)
XLA Modules:
  0.0 290.2 jit_solution(13539906217721251556)
XLA Ops:
  0.6 0.8 copy.12
  1.4 0.1 eq.29
  1.6 0.9 reduce-window.6
  2.5 0.2 slice_reduce_fusion
  2.7 0.1 eq.25
  2.9 0.1 fusion.1
  3.0 0.1 sub.7
  3.1 0.1 copy.15
  3.2 0.7 add_convert_fusion.1
  3.9 0.7 convert_element_type.28
  4.6 0.6 pad.4.info_own
  5.2 0.0 copy-start.3
  5.2 274.9 %expert_layer.1 = (bf16[192,3584]{1,0:T(8,128)(2,1)}, bf16[192,3584]{1,0:T(8,128)(2,1)}, f32[8,256]{1,0:T(8,128)}, f32[8,256]{1,0:T(8,128)}, bf16[896,1024]{1,0:...) custom-call(bf16[192,3584]{1,0:T(8,128)(2,1)} %tokens.1, bf16[192,3584]{1,0:T(8,128)(2,1)} %upstream.1, ...), custom_call_target="tpu_custom_call" | custom-call | tf_op jit(solution)/shard_map/expert_layer/pallas_call | solution.py:449
  280.1 0.0 copy-done.3
  280.1 1.3 fusion.5
  281.4 0.0 copy-start.2
  281.4 3.3 %add_convert_fusion = bf16[192,3584]{1,0:T(8,128)(2,1)} fusion(bf16[192,3584]{1,0:T(8,128)(2,1)} %get-tuple-element.13, bf16[192,3584]{1,0:T(8,128)(2,1)} %get-tuple-element.12), kind=kLoop, calls=%fused_computation | loop fusion | flops 2752512 | bytes 4128768 | tf_op jit(solution)/shard_map/convert_element_type | solution.py:471
  284.7 0.0 copy-done.2
  284.7 0.0 copy-start.1
  284.7 1.2 copy.21
  285.9 0.9 copy-done.1
  286.8 0.0 copy-start
  286.9 1.2 copy.22
  288.1 0.9 copy-done
  289.0 1.2 copy.23
  (4 shorter events, 0.1 us)
Async XLA Ops:
  5.2 274.9 %copy-start.3 = (bf16[192,2]{0,1:T(2,128)(2,1)S(1)}, bf16[192,2]{0,1:T(2,128)(2,1)}, u32[]{:S(2)}) copy-start(bf16[192,2]{0,1:T(2,128)(2,1)} %param.10) | copy-start | bytes 2308
  281.4 3.3 %copy-start.2 = (bf16[896,1024]{1,0:T(8,128)(2,1)S(1)}, bf16[896,1024]{1,0:T(8,128)(2,1)}, u32[]{:S(2)}) copy-start(bf16[896,1024]{1,0:T(8,128)(2,1)} %get-tuple-element.16) | copy-start | bytes 5505028
  284.7 2.2 copy-start.1
  286.8 2.2 copy-start

commit v4 on v3

v4 whole, which is shorter than its diff:
```python
import functools

import jax
import jax.numpy as jnp
from jax import lax
from jax.experimental import pallas as pl
from jax.experimental.pallas import tpu as pltpu
from jax.sharding import PartitionSpec as P

MESH = pl.DeviceIdType.MESH
ROWS = 16
PIECES = 1


def place():
    ep, plane = lax.axis_index("ep"), lax.axis_index("edp")
    core = lax.rem(ep, 2)
    parity = plane // 2
    beside = plane + 1 - 2 * lax.rem(plane, 2)
    across = 3 - plane
    return ep, ep // 2, core, plane, parity, beside, across


def remote(src, dst, send, recv, ep, plane):
    return pltpu.make_async_remote_copy(
        src_ref=src, dst_ref=dst, send_sem=send, recv_sem=recv,
        device_id=(ep, plane), device_id_type=MESH,
    )


def landed(ref, sem):
    pltpu.make_async_copy(ref, ref, sem).wait()


def layer_kernel(chips, tokens, upstream, ids_own, levels_own, w_gate, w_up, w_down,
                 token_out, gates_out, g_all,
                 x_all, dy_all, f_gate, f_up, f_down, slope, gated, act, d_gate, d_up, terms, arrived,
                 x_stage, dy_stage, gates_own, gates_in, gates_back, gates_mix, info_own, info_in,
                 mix_in, gates_mixed,
                 load_sem, swap_send, swap_recv, info_sem, stay_sem,
                 token_send, token_recv, hand_send, hand_recv, weight_send, weight_recv, away_recv, relay_send,
                 sum_send, sum_recv, pass_send, pass_recv, out_send, out_recv, back_send, back_recv,
                 mix_send, mix_recv):
    ep, chip, core, plane, parity, beside, across = place()
    depth, width = w_gate.shape
    half = width // 2
    tile = min(half, 256)
    parts = half // tile
    tok_count, model_width = tokens.shape
    tall = chips * ROWS
    sibling = ep + 1 - 2 * core
    away = core != parity
    weights = (w_gate, w_up, w_down)
    fulls = (f_gate, f_up, f_down)
    grads = [g_all.at[m] for m in range(3)]
    stages, alls = (x_stage, dy_stage), (x_all, dy_all)
    reply_back, reply_in = x_stage, dy_stage
    f32, bf16 = jnp.float32, jnp.bfloat16

    def rows_of(ref, shard):
        return ref.at[pl.ds(pl.multiple_of(shard * depth, 16), depth)]

    def columns(ref, part):
        return ref.at[:, pl.ds(pl.multiple_of(part * half, 128), half)]

    def strip(ref, part, n):
        return ref.at[:, pl.ds(pl.multiple_of(part * half + n * tile, 128), tile)]

    def shard_strip(m, shard, n):
        return strip(rows_of(fulls[m], shard), 0, n)

    def block(ref, group, index):
        return ref.at[group, pl.ds(pl.multiple_of(index * ROWS, ROWS), ROWS)]

    chunks = model_width // half
    fit = depth // tok_count
    slabs = -(-chunks // fit)

    def chunk_of(n, group, j):
        slab = slabs * (2 * n + group) + j // fit
        return terms.at[slab // 4, slab % 4, pl.ds(j % fit * tok_count, tok_count)]

    def source_of(n, j):
        return (tokens, upstream)[n].at[:, pl.ds(j * half, half)]

    def loads(n):
        return [pltpu.make_async_copy(source_of(n, j), chunk_of(n, 0, j), load_sem.at[n, j]) for j in range(chunks)]

    def swaps(n):
        return [remote(source_of(n, j), chunk_of(n, 1, j), swap_send.at[n, j], swap_recv.at[n, j], ep, across)
                for j in range(chunks)]

    def info_swap():
        return remote(info_own, info_in, info_sem.at[0], info_sem.at[1], ep, across)

    def hits(group):
        info = info_own if group == 0 else info_in
        ids = [info[k:k + 1, :tok_count] for k in range(2)]
        names = lax.broadcasted_iota(jnp.int32, (2 * chips, tok_count), 0).astype(f32)
        named = [names == one for one in ids]
        ones = [jnp.where(one, 1.0, 0.0) for one in named]
        earlier = (lax.broadcasted_iota(jnp.int32, (tok_count, tok_count), 0)
                   < lax.broadcasted_iota(jnp.int32, (tok_count, tok_count), 1))
        ranks = jnp.dot((ones[0] + ones[1]).astype(bf16), jnp.where(earlier, 1.0, 0.0).astype(bf16),
                        preferred_element_type=f32)
        rows = lax.broadcasted_iota(jnp.int32, (tall, tok_count), 0)
        slot = (rows + (rows // ROWS + parity) * ROWS).astype(f32)
        return [slot == ids[k] * ROWS + jnp.sum(ones[k] * ranks, axis=0, keepdims=True) for k in range(2)]

    def picks(n, group):
        info = info_own if group == 0 else info_in
        levels = [info[2 + k:3 + k, :tok_count] if n else jnp.ones((1, tok_count), f32) for k in range(2)]
        terms_of = [jnp.where(hit, level, 0.0) for hit, level in zip(hits(group), levels)]
        return (terms_of[0] + terms_of[1]).astype(bf16)

    def dispatch(n, group):
        chosen = picks(n, group)
        for j in range(chunks):
            rows = jnp.dot(chosen, chunk_of(n, group, j)[...], preferred_element_type=f32)
            stages[n][group, :, j * half:(j + 1) * half] = rows.astype(bf16)

    def stays(n, group):
        return pltpu.make_async_copy(block(stages[n], group, chip), block(alls[n].at[core], group, chip),
                                     stay_sem.at[n, group])

    def spread(n, group):
        def send(k, carry):
            to = lax.rem(chip + k, chips)
            remote(block(stages[n], group, to), block(alls[n].at[core], group, chip), token_send.at[n, group],
                   token_recv.at[n, group], 2 * to + core, plane).start()
            return carry

        stays(n, group).start()
        lax.fori_loop(1, chips, send, 0)

    def spread_done(n, group):
        stays(n, group).wait()
        landed(stages[n].at[group, pl.ds(0, (chips - 1) * ROWS)], token_send.at[n, group])

    size = depth // PIECES

    def piece(m, shard, n, r):
        return strip(fulls[m].at[pl.ds(pl.multiple_of(shard * depth + r * size, 16), size)], 0, n)

    def away_weights(m, n):
        @pl.when(away)
        def _():
            for part in range(2):
                for r in range(PIECES):
                    remote(strip(weights[m].at[pl.ds(r * size, size)], part, n), piece(m, plane, n, r),
                           weight_send.at[m, n, part], away_recv.at[m, n, r], 2 * chip + part, across).start()

    def home_weights(m, n):
        @pl.when(jnp.logical_not(away))
        def _():
            for part in range(2):
                remote(strip(weights[m], part, n), shard_strip(m, plane, n), weight_send.at[m, n, part],
                       weight_recv.at[m, n, 1], 2 * chip + part, beside).start()
            pltpu.make_async_copy(strip(weights[m], core, n), shard_strip(m, plane, n),
                                  weight_recv.at[m, n, 2]).start()
            remote(strip(weights[m], 1 - core, n), shard_strip(m, plane, n), weight_send.at[m, n, 2],
                   weight_recv.at[m, n, 2], sibling, plane).start()

    for n in range(2):
        for copy in loads(n):
            copy.start()
    barrier = pltpu.get_barrier_semaphore()
    info_own[...] = jnp.zeros(info_own.shape, f32)
    info_own[0:2, 0:tok_count] = ids_own[...].astype(f32)
    info_own[2:4, 0:tok_count] = levels_own[...].astype(f32)

    def greet(k, carry):
        pl.semaphore_signal(barrier, inc=1, device_id=(2 * lax.rem(chip + k, chips) + core, plane),
                            device_id_type=MESH)
        return carry

    lax.fori_loop(1, chips, greet, 0)
    for other in ((sibling, plane), (ep, across), (sibling, across), (ep, beside), (sibling, beside)):
        pl.semaphore_signal(barrier, inc=1, device_id=other, device_id_type=MESH)
    pl.semaphore_wait(barrier, chips + 4)

    info_swap().start()
    for n in range(2):
        for copy in swaps(n):
            copy.start()
        if n == 0:
            for m in range(3):
                home_weights(m, 0)
            away_weights(0, 0)
    for m in range(1, 3):
        away_weights(m, 0)
    for copy in loads(0):
        copy.wait()
    dispatch(0, 0)
    spread(0, 0)
    for copy in loads(1):
        copy.wait()
    dispatch(1, 0)
    spread(1, 0)
    for n in range(1, parts):
        for m in range(3):
            home_weights(m, n)
            away_weights(m, n)

    def start_relay(m, n):
        for r in range(PIECES):
            landed(piece(m, across, n, r), away_recv.at[m, n, r])
            remote(piece(m, across, n, r), piece(m, across, n, r), relay_send.at[m, n],
                   weight_recv.at[m, n, 0], 2 * chip + core, beside).start()

    def hand_over(n, group):
        return remote(alls[n].at[core, group], alls[n].at[core, group], hand_send.at[n, group],
                      hand_recv.at[n, group], sibling, plane)

    def pass_on(n, group):
        landed(alls[n].at[core, group, pl.ds(0, (chips - 1) * ROWS)], token_recv.at[n, group])
        spread_done(n, group)
        hand_over(n, group).start()

    def weights_here(m, n):
        landed(shard_strip(m, beside, n), weight_recv.at[m, n, 1])
        landed(shard_strip(m, plane, n), weight_recv.at[m, n, 2])
        landed(shard_strip(m, 3 - beside, n), weight_recv.at[m, n, 0])

    def product(left, k, group, right, cols):
        deep = min(model_width, 512)
        total = None
        for at in range(0, model_width, deep):
            term = jnp.dot(left[k, group, :, at:at + deep], right[at:at + deep, cols], preferred_element_type=f32)
            total = term if total is None else total + term
        return total

    def tiles(n):
        return pl.ds(pl.multiple_of(n * tile, tile), tile)

    def forward(n):
        cols = tiles(n)

        def step(i, carry):
            k, group = i // 2, lax.rem(i, 2)
            pre_gate = product(x_all, k, group, f_gate, cols)
            sigma = jax.nn.sigmoid(pre_gate)
            silu_val = pre_gate * sigma
            gated[k, group, :, cols] = silu_val
            slope[k, group, :, cols] = sigma * (1.0 + pre_gate * (1.0 - sigma))
            pre_up = product(x_all, k, group, f_up, cols)
            act[k, group, :, cols] = (gated[k, group, :, cols] * pre_up).astype(bf16)
            slope[k, group, :, cols] = slope[k, group, :, cols] * pre_up
            return carry

        lax.fori_loop(0, 4, step, 0)

    def backward(n):
        cols = tiles(n)

        def step(i, carry):
            k, group = i // 2, lax.rem(i, 2)
            back = product(dy_all, k, group, f_down, cols)
            d_gate[k, group, :, cols] = (back * slope[k, group, :, cols]).astype(bf16)
            d_up[k, group, :, cols] = (back * gated[k, group, :, cols]).astype(bf16)
            part = jnp.sum(act[k, group, :, cols].astype(f32) * back, axis=1, keepdims=True)
            whole = jnp.broadcast_to(part, gates_own.shape[2:])
            gates_own[k, group] = whole if n == 0 else gates_own[k, group] + whole
            return carry

        lax.fori_loop(0, 4, step, 0)

    def moved(m, i, n):
        return remote(strip(terms.at[m, i], 0, n), strip(arrived.at[m, i], 0, n), sum_send.at[m, i, n],
                      sum_recv.at[m, i, n], 2 * chip + core, beside)

    def gradients(i, n, sent):
        shard = jnp.where(i == 0, 3 - beside, jnp.where(i == 1, beside, jnp.where(i == 2, across, plane)))
        cols = pl.ds(pl.multiple_of(shard * depth, 128), depth)
        over = (((0,), (0,)), ((), ()))
        for m, left, right in ((0, x_all, d_gate), (1, x_all, d_up), (2, dy_all, act)):
            total = None
            for k in range(2):
                for group in range(2):
                    term = lax.dot_general(left[k, group, :, cols], right[k, group, :, tiles(n)], over,
                                           preferred_element_type=f32)
                    total = term if total is None else total + term
            terms[m, i, :, tiles(n)] = total.astype(bf16)
            if sent:
                moved(m, i, n).start()

    info_swap().wait()
    for copy in swaps(0):
        copy.wait_recv()
    dispatch(0, 1)
    spread(0, 1)
    pass_on(0, 0)
    for copy in swaps(1):
        copy.wait_recv()
    dispatch(1, 1)
    start_relay(0, 0)
    pass_on(0, 1)
    spread(1, 1)
    start_relay(1, 0)
    pass_on(1, 0)
    start_relay(2, 0)
    pass_on(1, 1)
    for n in range(parts):
        for m in range(2):
            weights_here(m, n)
        if n == 0:
            for group in range(2):
                landed(x_all.at[1 - core, group], hand_recv.at[0, group])
        forward(n)
        if n + 1 < parts:
            start_relay(0, n + 1)
        weights_here(2, n)
        if n == 0:
            for group in range(2):
                landed(dy_all.at[1 - core, group], hand_recv.at[1, group])
        backward(n)
        if n + 1 < parts:
            start_relay(1, n + 1)
            start_relay(2, n + 1)

        def first(i, carry, n=n):
            gradients(i, n, True)
            return carry

        lax.fori_loop(0, 2, first, 0)

    def rest(i, carry):
        gradients(2 + i // parts, lax.rem(i, parts), False)
        return carry

    lax.fori_loop(0, 2 * parts, rest, 0)

    for n in range(2):
        for group in range(2):
            hand_over(n, group).wait_send()

    def replies(k, group, other):
        wide = min(model_width, 512)

        def step(n, carry):
            cols = pl.ds(pl.multiple_of(n * wide, wide), wide)
            contract = (((1,), (1,)), ((), ()))
            total = lax.dot_general(d_gate[k, group], f_gate[cols], contract, preferred_element_type=f32)
            total = total + lax.dot_general(d_up[k, group], f_up[cols], contract, preferred_element_type=f32)
            if other is not None:
                total = total + other[group, :, cols].astype(f32)
            x_all[k, group, :, cols] = total.astype(bf16)
            return carry

        lax.fori_loop(0, model_width // wide, step, 0)

    gates_pass = remote(gates_own.at[1 - core], gates_in, pass_send.at[2], pass_recv.at[2], sibling, plane)
    gates_pass.start()

    def reply_pass(group):
        return remote(x_all.at[1 - core, group], reply_in.at[group], pass_send.at[group], pass_recv.at[group],
                      sibling, plane)

    for group in (1, 0):
        replies(1 - core, group, None)
        reply_pass(group).start()
    gates_pass.wait()
    gates_own[core] = gates_own[core] + gates_in[...]
    for group in (1, 0):
        reply_pass(group).wait()
        replies(core, group, reply_in)

        def send(k, carry, group=group):
            to = lax.rem(chip + k, chips)
            for n, (own, back) in enumerate(((x_all, reply_back), (gates_own, gates_back))):
                remote(block(own.at[core], group, to), block(back, group, chip), back_send.at[n, group],
                       back_recv.at[n, group], 2 * to + core, plane).start()
            return carry

        for n, (own, back) in enumerate(((x_all, reply_back), (gates_own, gates_back))):
            pltpu.make_async_copy(block(own.at[core], group, chip), block(back, group, chip),
                                  back_recv.at[n, group]).start()
        lax.fori_loop(1, chips, send, 0)

    def combine(group):
        landed(reply_back.at[group], back_recv.at[0, group])
        landed(gates_back.at[group], back_recv.at[1, group])
        chosen = picks(0, group)
        for j in range(chunks):
            cols = slice(j * half, (j + 1) * half)
            total = lax.dot_general(chosen, reply_back[group, :, cols], (((0,), (0,)), ((), ())),
                                    preferred_element_type=f32)
            dy_all[0, group, 0:tok_count, cols] = total.astype(bf16)
        gates_mix[group] = jnp.zeros(gates_mix.shape[1:], f32)
        for k, hit in enumerate(hits(group)):
            values = jnp.where(hit, gates_back[group, :, 0:1], 0.0)
            gates_mix[group, k:k + 1, 0:tok_count] = jnp.sum(values, axis=0, keepdims=True)

    def mixed(group):
        if group == 0:
            return []
        rows = dy_all.at[0, 1, pl.ds(0, tok_count)]
        return [remote(rows, mix_in, mix_send.at[1, 0], mix_recv.at[0], ep, across),
                remote(gates_mix.at[1], gates_mixed, mix_send.at[1, 1], mix_recv.at[1], ep, across)]

    for n in range(parts):
        if n == parts - 1:
            for group in (1, 0):
                combine(group)
                for copy in mixed(group):
                    copy.start()
        for i in range(2):
            for m in range(3):
                moved(m, i, n).wait()
                step = 128

                def add(k, carry, m=m, i=i, n=n):
                    rows = pl.ds(pl.multiple_of(k * step, step), step)
                    total = terms[m, 2 + i, rows, tiles(n)].astype(f32) + arrived[m, i, rows, tiles(n)].astype(f32)
                    terms[m, 2 + i, rows, tiles(n)] = total.astype(bf16)
                    return carry

                lax.fori_loop(0, depth // step, add, 0)
                done, out = strip(terms.at[m, 2 + i], 0, n), strip(grads[m], core, n)
                if i == 0:
                    remote(done, out, out_send.at[m, 0, n], out_recv.at[m, core, n],
                           2 * chip + parity, across).start()
                else:
                    @pl.when(core == parity)
                    def _(m=m, n=n, done=done, out=out):
                        pltpu.make_async_copy(done, out, out_recv.at[m, core, n]).start()

                    @pl.when(core != parity)
                    def _(m=m, n=n, done=done, out=out):
                        remote(done, out, out_send.at[m, 1, n], out_recv.at[m, core, n],
                               2 * chip + parity, plane).start()

    for copy in mixed(1):
        copy.wait()
    mix_own = dy_all.at[0, 0]
    for j in range(chunks):
        cols = slice(j * half, (j + 1) * half)
        total = mix_own[0:tok_count, cols].astype(f32) + mix_in[:, cols].astype(f32)
        mix_in[:, cols] = total.astype(bf16)
    for k in range(2):
        gates_mix[0, k:k + 1, 0:tok_count] = gates_mix[0, k:k + 1, 0:tok_count] + gates_mixed[k:k + 1, 0:tok_count]
    finals = [pltpu.make_async_copy(mix_in, token_out, mix_send.at[0, 0]),
              pltpu.make_async_copy(gates_mix.at[0], gates_out, mix_send.at[0, 1])]
    for copy in finals:
        copy.start()

    for n in range(parts):
        for m in range(3):
            landed(shard_strip(m, across, n), relay_send.at[m, n])
            for part in range(2):
                landed(strip(weights[m], part, n), weight_send.at[m, n, part])

            @pl.when(jnp.logical_not(away))
            def _(m=m, n=n):
                landed(strip(weights[m], 0, n), weight_send.at[m, n, 2])
            landed(strip(terms.at[m, 2], 0, n), out_send.at[m, 0, n])

            @pl.when(core != parity)
            def _(m=m, n=n):
                landed(strip(terms.at[m, 3], 0, n), out_send.at[m, 1, n])
            for part in range(2):
                landed(strip(grads[m], part, n), out_recv.at[m, part, n])
    for n in range(2):
        for copy in swaps(n):
            copy.wait_send()
    for n, own in enumerate((x_all, gates_own)):
        for group in range(2):
            landed(own.at[core, group, pl.ds(0, (chips - 1) * ROWS)], back_send.at[n, group])
    for copy in finals:
        copy.wait()


def shards(tokens, upstream, expert_ids, gate_values, w_gate, w_up, w_down):
    experts = lax.axis_size("ep")
    chips = experts // 2
    tok_count, top_count = expert_ids.shape
    model_width = tokens.shape[1]
    depth, width = w_gate.shape[1:]
    half = width // 2
    bf16 = jnp.bfloat16
    lanes = -(-tok_count // 128) * 128
    anywhere = pl.BlockSpec(memory_space=pl.ANY)
    dma = pltpu.SemaphoreType.DMA
    tall = chips * ROWS
    rows_buffer = pltpu.VMEM((2, 2, tall, model_width), bf16)
    full_buffer = pltpu.VMEM((4 * depth, half), bf16)
    wide_buffer = pltpu.VMEM((2, 2, tall, half), jnp.float32)
    narrow_buffer = pltpu.VMEM((2, 2, tall, half), bf16)
    grad_shape = jax.ShapeDtypeStruct((3, depth, width), bf16)
    mix_shape = jax.ShapeDtypeStruct((tok_count, model_width), bf16)
    info_shape = jax.ShapeDtypeStruct((8, lanes), jnp.float32)
    parts = max(1, half // 256)
    token_grad, gate_grad, grads = pl.pallas_call(
        functools.partial(layer_kernel, chips),
        out_shape=[mix_shape, info_shape, grad_shape],
        in_specs=[anywhere] * 2 + [pl.BlockSpec(memory_space=pltpu.VMEM)] * 2 + [anywhere] * 3,
        out_specs=[anywhere] * 3,
        scratch_shapes=[
            rows_buffer, rows_buffer, full_buffer, full_buffer, full_buffer,
            wide_buffer, wide_buffer, narrow_buffer, narrow_buffer, narrow_buffer,
            pltpu.VMEM((3, 4, depth, half), bf16), pltpu.VMEM((3, 2, depth, half), bf16),
            pltpu.VMEM((2, tall, model_width), bf16), pltpu.VMEM((2, tall, model_width), bf16),
            pltpu.VMEM((2, 2, tall, 128), jnp.float32), pltpu.VMEM((2, tall, 128), jnp.float32),
            pltpu.VMEM((2, tall, 128), jnp.float32), pltpu.VMEM((2, 8, lanes), jnp.float32),
            pltpu.VMEM((8, lanes), jnp.float32), pltpu.VMEM((8, lanes), jnp.float32), pltpu.VMEM((tok_count, model_width), bf16),
            pltpu.VMEM((8, lanes), jnp.float32),
            dma((2, model_width // half)), dma((2, model_width // half)), dma((2, model_width // half)),
            dma((2,)), dma((2, 2)),
            dma((2, 2)), dma((2, 2)), dma((2, 2)), dma((2, 2)),
            dma((3, parts, 3)), dma((3, parts, 3)), dma((3, parts, PIECES)), dma((3, parts)),
            dma((3, 2, parts)), dma((3, 2, parts)), dma((3,)), dma((3,)), dma((3, 2, parts)), dma((3, 2, parts)),
            dma((2, 2)), dma((2, 2)),
            dma((2, 2)), dma((2,))],
        compiler_params=pltpu.CompilerParams(has_side_effects=True, collective_id=0, vmem_limit_bytes=60 << 20),
        name="expert_layer",
    )(tokens, upstream, expert_ids.T, gate_values.T, w_gate[0], w_up[0], w_down[0])

    gate_grad = gate_grad[:top_count, :tok_count].T
    gate_grad = (gate_grad / gate_values.astype(jnp.float32)).astype(bf16)
    return token_grad, gate_grad, grads[0:1], grads[1:2], grads[2:3]


def solution(mesh):
    tokens_spec, weights_spec = P(("ep", "edp"), None), P("ep", "edp", None)
    return jax.shard_map(
        shards, mesh=mesh,
        in_specs=(tokens_spec,) * 4 + (weights_spec,) * 3,
        out_specs=(tokens_spec,) * 2 + (weights_spec,) * 3,
        check_vma=False,
    )
```

time: 291 us -> 282 us (0.969)
  other arithmetic: 6.99 us -> 1.27 us
    unnamed x12 -> x5, local copies, waits for them, and re-layouts: 6.35 us -> 1.09 us
    slice x1, local copies, waits for them, and re-layouts: 0.22 us -> 5.29 us  [shards(): return (token_grad, gate_grad, grads[0:1], grads[1:2], grads[2:3])]
    convert_element_type x4 -> x0, other arithmetic: 4.67 us -> none  [the longest x1 3.28 us: shards(): (mix_own.astype(jnp.float32) + mix_across.astype(jnp.float32)).astype(bf16)]
where the time goes in v4:
time: 282 us; the launch traced here: 281 us
  Pallas kernels  273 us (97%)
  local copies, waits for them, and re-layouts  6.38 us (2%)
    pallas_call x1, Pallas kernels, shards(): pl.pallas_call(functools.partial(layer_kernel, chips), out_shape=[mix_sha...  273 us

profile of v4, /device:TPU:112, one launch (start us, length us, event | category | flops | bytes accessed | tf_op | source)
XLA Modules:
  0.0 281.0 jit_solution(8766681494222824724)
XLA Ops:
  0.6 0.0 copy-start.1
  0.6 272.7 %expert_layer.1 = (bf16[192,3584]{1,0:T(8,128)(2,1)}, f32[8,256]{1,0:T(8,128)}, bf16[3,896,1024]{2,1,0:T(8,128)(2,1)}) custom-call(bf16[192,3584]{1,0:T(8,128)(2,1)} %tokens.1, bf16[192,3584]{1,0:T(8,128)(2,1)} %upstream.1, s32[2,192]{1,0:T(2,128)} %bitcast.13, bf16[2,192]{1,0:T(2,128)(2,1)} %bitcast.12, bf16[896,1024]{1,0:T(8,128)(2,1)} %bitcast.9, ...), custom_call_target="tpu_custom_call" | custom-call | tf_op jit(solution)/shard_map/expert_layer/pallas_call | solution.py:493
  273.4 0.0 copy-done.1
  273.4 1.3 fusion
  274.7 0.0 copy-start
  274.7 5.3 %fusion.1 = (bf16[1,896,1024]{2,1,0:T(8,128)(2,1)}, bf16[1,896,1024]{2,1,0:T(8,128)(2,1)}, bf16[1,896,1024]{2,1,0:T(8,128)(2,1)}) fusion(bf16[3,896,1024]{2,1,0:T(8,128)(2,1)} %get-tuple-element.10), kind=kLoop, calls=%fused_computation.2 | loop fusion | bytes 11010048 | tf_op jit(solution)/shard_map/slice | solution.py:520
  280.0 0.0 copy-done
  280.0 1.1 copy.13
Async XLA Ops:
  0.6 272.8 %copy-start.1 = (bf16[192,2]{0,1:T(2,128)(2,1)S(1)}, bf16[192,2]{0,1:T(2,128)(2,1)}, u32[]{:S(2)}) copy-start(bf16[192,2]{0,1:T(2,128)(2,1)} %param.10) | copy-start | bytes 2308
  274.7 5.3 %copy-start = (bf16[192,3584]{1,0:T(8,128)(2,1)S(1)}, bf16[192,3584]{1,0:T(8,128)(2,1)}, u32[]{:S(2)}) copy-start(bf16[192,3584]{1,0:T(8,128)(2,1)} %get-tuple-element.19) | copy-start | bytes 4128772

commit v5 on v4

--- a/solution.py
+++ b/solution.py
@@ -183,12 +183,6 @@
     for n in range(2):
         for copy in swaps(n):
             copy.start()
-        if n == 0:
-            for m in range(3):
-                home_weights(m, 0)
-            away_weights(0, 0)
-    for m in range(1, 3):
-        away_weights(m, 0)
     for copy in loads(0):
         copy.wait()
     dispatch(0, 0)
@@ -197,6 +191,9 @@
         copy.wait()
     dispatch(1, 0)
     spread(1, 0)
+    for m in range(3):
+        home_weights(m, 0)
+        away_weights(m, 0)
     for n in range(1, parts):
         for m in range(3):
             home_weights(m, n)
@@ -405,6 +402,20 @@
                 for copy in mixed(group):
                     copy.start()
         for i in range(2):
+            if i == 1 and n == parts - 1:
+                for copy in mixed(1):
+                    copy.wait()
+                mix_own = dy_all.at[0, 0]
+                for j in range(chunks):
+                    cols = slice(j * half, (j + 1) * half)
+                    total = mix_own[0:tok_count, cols].astype(f32) + mix_in[:, cols].astype(f32)
+                    mix_in[:, cols] = total.astype(bf16)
+                for k in range(2):
+                    gates_mix[0, k:k + 1, 0:tok_count] = gates_mix[0, k:k + 1, 0:tok_count] + gates_mixed[k:k + 1, 0:tok_count]
+                finals = [pltpu.make_async_copy(mix_in, token_out, mix_send.at[0, 0]),
+                          pltpu.make_async_copy(gates_mix.at[0], gates_out, mix_send.at[0, 1])]
+                for copy in finals:
+                    copy.start()
             for m in range(3):
                 moved(m, i, n).wait()
                 step = 128
@@ -429,20 +440,6 @@
                     def _(m=m, n=n, done=done, out=out):
                         remote(done, out, out_send.at[m, 1, n], out_recv.at[m, core, n],
                                2 * chip + parity, plane).start()
-
-    for copy in mixed(1):
-        copy.wait()
-    mix_own = dy_all.at[0, 0]
-    for j in range(chunks):
-        cols = slice(j * half, (j + 1) * half)
-        total = mix_own[0:tok_count, cols].astype(f32) + mix_in[:, cols].astype(f32)
-        mix_in[:, cols] = total.astype(bf16)
-    for k in range(2):
-        gates_mix[0, k:k + 1, 0:tok_count] = gates_mix[0, k:k + 1, 0:tok_count] + gates_mixed[k:k + 1, 0:tok_count]
-    finals = [pltpu.make_async_copy(mix_in, token_out, mix_send.at[0, 0]),
-              pltpu.make_async_copy(gates_mix.at[0], gates_out, mix_send.at[0, 1])]
-    for copy in finals:
-        copy.start()
 
     for n in range(parts):
         for m in range(3):

time: 282 us -> 280 us (level)
  no operation moved by 1% of the time
where the time goes in v5:
time: 280 us
  Pallas kernels  272 us (97%)
  local copies, waits for them, and re-layouts  6.38 us (2%)
    pallas_call x1, Pallas kernels, shards(): pl.pallas_call(functools.partial(layer_kernel, chips), out_shape=[mix_sha...  272 us

profile of v5, /device:TPU:112, one launch (start us, length us, event | category | flops | bytes accessed | tf_op | source)
XLA Modules:
  0.0 280.3 jit_solution(5025424990411927090)
XLA Ops:
  0.6 0.0 copy-start.1
  0.6 271.9 %expert_layer.1 = (bf16[192,3584]{1,0:T(8,128)(2,1)}, f32[8,256]{1,0:T(8,128)}, bf16[3,896,1024]{2,1,0:T(8,128)(2,1)}) custom-call(bf16[192,3584]{1,0:T(8,128)(2,1)} %tokens.1, bf16[192,3584]{1,0:T(8,128)(2,1)} %upstream.1, s32[2,192]{1,0:T(2,128)} %bitcast.13, bf16[2,192]{1,0:T(2,128)(2,1)} %bitcast.12, bf16[896,1024]{1,0:T(8,128)(2,1)} %bitcast.9, ...), custom_call_target="tpu_custom_call" | custom-call | tf_op jit(solution)/shard_map/expert_layer/pallas_call | solution.py:490
  272.6 0.0 copy-done.1
  272.6 1.3 fusion
  273.9 0.0 copy-start
  273.9 5.3 %fusion.1 = (bf16[1,896,1024]{2,1,0:T(8,128)(2,1)}, bf16[1,896,1024]{2,1,0:T(8,128)(2,1)}, bf16[1,896,1024]{2,1,0:T(8,128)(2,1)}) fusion(bf16[3,896,1024]{2,1,0:T(8,128)(2,1)} %get-tuple-element.10), kind=kLoop, calls=%fused_computation.2 | loop fusion | bytes 11010048 | tf_op jit(solution)/shard_map/slice | solution.py:517
  279.2 0.0 copy-done
  279.2 1.1 copy.13
Async XLA Ops:
  0.6 272.0 %copy-start.1 = (bf16[192,2]{0,1:T(2,128)(2,1)S(1)}, bf16[192,2]{0,1:T(2,128)(2,1)}, u32[]{:S(2)}) copy-start(bf16[192,2]{0,1:T(2,128)(2,1)} %param.10) | copy-start | bytes 2308
  273.9 5.3 %copy-start = (bf16[192,3584]{1,0:T(8,128)(2,1)S(1)}, bf16[192,3584]{1,0:T(8,128)(2,1)}, u32[]{:S(2)}) copy-start(bf16[192,3584]{1,0:T(8,128)(2,1)} %get-tuple-element.19) | copy-start | bytes 4128772

commit v6 on v5

--- a/solution.py
+++ b/solution.py
@@ -161,13 +161,7 @@
             remote(strip(weights[m], 1 - core, n), shard_strip(m, plane, n), weight_send.at[m, n, 2],
                    weight_recv.at[m, n, 2], sibling, plane).start()
 
-    for n in range(2):
-        for copy in loads(n):
-            copy.start()
     barrier = pltpu.get_barrier_semaphore()
-    info_own[...] = jnp.zeros(info_own.shape, f32)
-    info_own[0:2, 0:tok_count] = ids_own[...].astype(f32)
-    info_own[2:4, 0:tok_count] = levels_own[...].astype(f32)
 
     def greet(k, carry):
         pl.semaphore_signal(barrier, inc=1, device_id=(2 * lax.rem(chip + k, chips) + core, plane),
@@ -177,6 +171,13 @@
     lax.fori_loop(1, chips, greet, 0)
     for other in ((sibling, plane), (ep, across), (sibling, across), (ep, beside), (sibling, beside)):
         pl.semaphore_signal(barrier, inc=1, device_id=other, device_id_type=MESH)
+    for n in range(2):
+        for copy in loads(n):
+            copy.start()
+    info_own[...] = jnp.zeros(info_own.shape, f32)
+    info_own[0:2, 0:tok_count] = ids_own[...].astype(f32)
+    info_own[2:4, 0:tok_count] = levels_own[...].astype(f32)
+
     pl.semaphore_wait(barrier, chips + 4)
 
     info_swap().start()

time: 280 us -> 282 us (level); the launches traced: 280 us -> 279 us
  no operation moved by 1% of the time
where the time goes in v6:
time: 282 us; the launch traced here: 279 us
  Pallas kernels  271 us (96%)
  local copies, waits for them, and re-layouts  6.38 us (2%)
    pallas_call x1, Pallas kernels, shards(): pl.pallas_call(functools.partial(layer_kernel, chips), out_shape=[mix_sha...  271 us

profile of v6, /device:TPU:112, one launch (start us, length us, event | category | flops | bytes accessed | tf_op | source)
XLA Modules:
  0.0 278.9 jit_solution(2323259762222561669)
XLA Ops:
  0.6 0.0 copy-start.1
  0.6 270.6 %expert_layer.1 = (bf16[192,3584]{1,0:T(8,128)(2,1)}, f32[8,256]{1,0:T(8,128)}, bf16[3,896,1024]{2,1,0:T(8,128)(2,1)}) custom-call(bf16[192,3584]{1,0:T(8,128)(2,1)} %tokens.1, bf16[192,3584]{1,0:T(8,128)(2,1)} %upstream.1, s32[2,192]{1,0:T(2,128)} %bitcast.13, bf16[2,192]{1,0:T(2,128)(2,1)} %bitcast.12, bf16[896,1024]{1,0:T(8,128)(2,1)} %bitcast.9, ...), custom_call_target="tpu_custom_call" | custom-call | tf_op jit(solution)/shard_map/expert_layer/pallas_call | solution.py:491
  271.2 0.0 copy-done.1
  271.3 1.3 fusion
  272.5 0.0 copy-start
  272.5 5.3 %fusion.1 = (bf16[1,896,1024]{2,1,0:T(8,128)(2,1)}, bf16[1,896,1024]{2,1,0:T(8,128)(2,1)}, bf16[1,896,1024]{2,1,0:T(8,128)(2,1)}) fusion(bf16[3,896,1024]{2,1,0:T(8,128)(2,1)} %get-tuple-element.10), kind=kLoop, calls=%fused_computation.2 | loop fusion | bytes 11010048 | tf_op jit(solution)/shard_map/slice | solution.py:518
  277.8 0.0 copy-done
  277.8 1.1 copy.13
Async XLA Ops:
  0.6 270.6 %copy-start.1 = (bf16[192,2]{0,1:T(2,128)(2,1)S(1)}, bf16[192,2]{0,1:T(2,128)(2,1)}, u32[]{:S(2)}) copy-start(bf16[192,2]{0,1:T(2,128)(2,1)} %param.10) | copy-start | bytes 2308
  272.5 5.3 %copy-start = (bf16[192,3584]{1,0:T(8,128)(2,1)S(1)}, bf16[192,3584]{1,0:T(8,128)(2,1)}, u32[]{:S(2)}) copy-start(bf16[192,3584]{1,0:T(8,128)(2,1)} %get-tuple-element.19) | copy-start | bytes 4128772
